TPU v7x, 32 devices: a whole 2x2x4 slice. The times are simulated.
32 devices in a mesh: tm: 4 (over z), sx: 4 (over y, x), sy: 2 (over core).
Axes of the slice: x: 2, y: 2, z: 4, core: 2. Of those that a mesh axis runs over, the one named last changes fastest.
Arguments:
- sources: float32 [8, 32, 32, 128], P('tm', 'sx', 'sy'), may hold values from -6 to 6
- forward_states: float32 [8, 32, 32, 128], P('tm', 'sx', 'sy'), may hold values from -6 to 6
- terminal: float32 [32, 32, 128], P('sx', 'sy'), may hold values from -6 to 6
- damping: float32 [32, 32, 128], P('sx', 'sy'), may hold values from 0.001 to 0.1
- contact_stiff: float32 [8], replicated, may hold values from 0.001 to 1
- regions: int32 [8, 4, 4], P('tm', 'sx', 'sy'), may hold values from 0 to 7
Outputs:
- adjoint: float32 [8, 32, 32, 128], P('tm', 'sx', 'sy')
- damping_grad: float32 [32, 32, 128], P('sx', 'sy')
Inputs may be any that keep to these rules, and one draw needn't show every extreme that they name: `regions`: region of a block of 8 x 8 columns of cells at a step.
All inputs are finite; a program needn't handle non-finite values.
Results may differ from a plain program's by a relative error of at most 0.0003.
Values sent between devices are 32-bit elements; how exact they have to be, the bound alone decides.
A program may use at most 64 MiB of HBM per device.

v0:
```python
import jax
import jax.numpy as jnp
from jax import lax
from jax.sharding import PartitionSpec as P

SWEEPS = 4
REGIONS = 8
BLOCK_CELLS = 8


coupling = 0.5


def with_halo(array, sides, width):
    for axis, dim in sides:
        count, length = (lax.axis_size(axis), array.shape[dim])
        up = [(i, (i + 1) % count) for i in range(count - 1)]
        down = [(j, i) for i, j in up]
        last = lax.slice_in_dim(array, length - width, length, axis=dim)
        leading = lax.slice_in_dim(array, 0, width, axis=dim)
        before = lax.ppermute(last, axis, up)
        after = lax.ppermute(leading, axis, down)
        array = jnp.concatenate([before, array, after], axis=dim)
    return array


def passed_along(value, axis, steps):
    count = lax.axis_size(axis)
    leading, last = (max(0, -steps), min(count, count - steps))
    return lax.ppermute(value, axis, [(source, source + steps) for source in range(leading, last)])


def neighbours(field):
    extended = with_halo(field, (("sx", 0), ("sy", 1)), 1)
    padded = jnp.pad(extended, ((0, 0), (0, 0), (1, 1)))
    total = padded[2:, 1:-1, 1:-1] + padded[:-2, 1:-1, 1:-1]
    total = total + padded[1:-1, 2:, 1:-1] + padded[1:-1, :-2, 1:-1]
    total = total + padded[1:-1, 1:-1, 2:] + padded[1:-1, 1:-1, :-2]
    return total


def propagate(right, diagonal):
    field = right
    for sweep_index in range(SWEEPS):
        field = (right + coupling * neighbours(field)) / diagonal
    return field


def reaction(region_ids, contact_stiff, damping):
    labels = jnp.arange(REGIONS, dtype=jnp.int32)
    picked = jnp.sum(
        jnp.where(region_ids[:, :, None] == labels, contact_stiff, jnp.zeros_like(contact_stiff)),
        axis=2,
    )
    spread = jnp.repeat(jnp.repeat(picked, BLOCK_CELLS, axis=0), BLOCK_CELLS, axis=1)
    return spread[:, :, None] + damping


def shards(sources, forward_states, terminal, damping, contact_stiff, regions):
    steps_here = sources.shape[0]
    slab_index = lax.axis_index("tm")
    last_slab = slab_index == lax.axis_size("tm") - 1
    zeros_field = jnp.zeros_like(terminal)
    reactions = [
        reaction(regions[position], contact_stiff, damping) for position in range(steps_here)
    ]
    diagonals = [1.0 + reactions[position] + 6.0 * coupling for position in range(steps_here)]
    field = jnp.where(last_slab, terminal, zeros_field)
    for position in range(steps_here - 1, -1, -1):
        field = propagate(field, diagonals[position]) + sources[position]
    coarse_rhs = field
    factor = 1.0 / (1.0 + steps_here * reactions[0])

    def advance(iteration, value):
        return factor * passed_along(value, "tm", -1) + coarse_rhs

    corrected = lax.fori_loop(0, lax.axis_size("tm") - 1, advance, coarse_rhs)
    incoming = passed_along(corrected, "tm", -1)
    field = jnp.where(last_slab, terminal, incoming)
    layers = [corrected] * steps_here
    position = 1
    field = propagate(field, diagonals[position]) + sources[position]
    layers[position] = field
    adjoint = jnp.stack(layers)
    partial_grad = jnp.sum(adjoint * forward_states, axis=0)
    damping_grad = -lax.psum(partial_grad, "tm")
    return (adjoint, damping_grad)


def solution(mesh):
    in_specs = (
        P("tm", "sx", "sy", None),
        P("tm", "sx", "sy", None),
        P("sx", "sy", None),
        P("sx", "sy", None),
        P(),
        P("tm", "sx", "sy"),
    )
    out_specs = (P("tm", "sx", "sy", None), P("sx", "sy", None))
    return jax.shard_map(shards, mesh=mesh, in_specs=in_specs, out_specs=out_specs, check_vma=False)
```

profile of v0, /device:TPU:0, one launch (start us, length us, event | category | flops | bytes accessed | tf_op | source)
XLA Modules:
  0.0 249.4 jit_solution(977297166873843467)
XLA Ops:
  8.6 5.5 %collective-permute-start.2 = (f32[1,16,128]{2,1,0:T(8,128)S(1)}, f32[1,16,128]{2,1,0:T(8,128)S(1)}, u32[]{:S(2)}, u32[]{:S(2)}) collective-permute-start(f32[1,16,128]{2,1,0:T(8,128)S(1)} %get-tuple-element.85), channel_id=1, source_target_pairs={{0,2},{2,4},{4,6},{1,3},{3,5},{5,7},{8,10},{10,12},{12,14},{9,11},... | collective-permute-start | bytes 24584 | tf_op jit(solution)/shard_map/ppermute | solution.py:21
  16.7 3.0 %collective-permute-start.4 = (f32[10,1,128]{2,1,0:T(1,128)S(1)}, f32[10,1,128]{2,1,0:T(1,128)S(1)}, u32[]{:S(2)}, u32[]{:S(2)}) collective-permute-start(f32[10,1,128]{2,1,0:T(1,128)S(1)} %get-tuple-element.59), channel_id=1, source_target_pairs={{0,1},{2,3},{4,5},{6,7},{8,9},{10,11},{12,13},{14,15},{16,17},{18,... | collective-permute-start | bytes 15368 | tf_op jit(solution)/shard_map/ppermute | solution.py:21
  23.0 5.4 %collective-permute-start.6 = (f32[1,16,128]{2,1,0:T(8,128)S(1)}, f32[1,16,128]{2,1,0:T(8,128)S(1)}, u32[]{:S(2)}, u32[]{:S(2)}) collective-permute-start(f32[1,16,128]{2,1,0:T(8,128)S(1)} %get-tuple-element.83), channel_id=1, source_target_pairs={{0,2},{2,4},{4,6},{1,3},{3,5},{5,7},{8,10},{10,12},{12,14},{9,11},... | collective-permute-start | bytes 24584 | tf_op jit(solution)/shard_map/ppermute | solution.py:21
  31.1 3.2 %collective-permute-start.8 = (f32[10,1,128]{2,1,0:T(1,128)S(1)}, f32[10,1,128]{2,1,0:T(1,128)S(1)}, u32[]{:S(2)}, u32[]{:S(2)}) collective-permute-start(f32[10,1,128]{2,1,0:T(1,128)S(1)} %get-tuple-element.57), channel_id=1, source_target_pairs={{0,1},{2,3},{4,5},{6,7},{8,9},{10,11},{12,13},{14,15},{16,17},{18,... | collective-permute-start | bytes 15368 | tf_op jit(solution)/shard_map/ppermute | solution.py:21
  35.4 5.1 %collective-permute-start.10 = (f32[1,16,128]{2,1,0:T(8,128)S(1)}, f32[1,16,128]{2,1,0:T(8,128)S(1)}, u32[]{:S(2)}, u32[]{:S(2)}) collective-permute-start(f32[1,16,128]{2,1,0:T(8,128)S(1)} %get-tuple-element.81), channel_id=1, source_target_pairs={{0,2},{2,4},{4,6},{1,3},{3,5},{5,7},{8,10},{10,12},{12,14},{9,11},... | collective-permute-start | bytes 24584 | tf_op jit(solution)/shard_map/ppermute | solution.py:21
  41.9 5.4 %collective-permute-done.9 = f32[1,16,128]{2,1,0:T(8,128)S(1)} collective-permute-done((f32[1,16,128]{2,1,0:T(8,128)S(1)}, f32[1,16,128]{2,1,0:T(8,128)S(1)}, u32[]{:S(2)}, u32[]{:S(2)}) %collective-permute-start.9) | collective-permute-done | bytes 8224 | tf_op jit(solution)/shard_map/ppermute | solution.py:22
  48.6 3.0 %collective-permute-start.12 = (f32[10,1,128]{2,1,0:T(1,128)S(1)}, f32[10,1,128]{2,1,0:T(1,128)S(1)}, u32[]{:S(2)}, u32[]{:S(2)}) collective-permute-start(f32[10,1,128]{2,1,0:T(1,128)S(1)} %get-tuple-element.55), channel_id=1, source_target_pairs={{0,1},{2,3},{4,5},{6,7},{8,9},{10,11},{12,13},{14,15},{16,17},{18,... | collective-permute-start | bytes 15368 | tf_op jit(solution)/shard_map/ppermute | solution.py:21
  54.0 5.4 %collective-permute-start.14 = (f32[1,16,128]{2,1,0:T(8,128)S(1)}, f32[1,16,128]{2,1,0:T(8,128)S(1)}, u32[]{:S(2)}, u32[]{:S(2)}) collective-permute-start(f32[1,16,128]{2,1,0:T(8,128)S(1)} %get-tuple-element.79), channel_id=1, source_target_pairs={{0,2},{2,4},{4,6},{1,3},{3,5},{5,7},{8,10},{10,12},{12,14},{9,11},... | collective-permute-start | bytes 24584 | tf_op jit(solution)/shard_map/ppermute | solution.py:21
  62.1 3.2 %collective-permute-start.16 = (f32[10,1,128]{2,1,0:T(1,128)S(1)}, f32[10,1,128]{2,1,0:T(1,128)S(1)}, u32[]{:S(2)}, u32[]{:S(2)}) collective-permute-start(f32[10,1,128]{2,1,0:T(1,128)S(1)} %get-tuple-element.53), channel_id=1, source_target_pairs={{0,1},{2,3},{4,5},{6,7},{8,9},{10,11},{12,13},{14,15},{16,17},{18,... | collective-permute-start | bytes 15368 | tf_op jit(solution)/shard_map/ppermute | solution.py:21
  67.7 5.4 %collective-permute-start.18 = (f32[1,16,128]{2,1,0:T(8,128)S(1)}, f32[1,16,128]{2,1,0:T(8,128)S(1)}, u32[]{:S(2)}, u32[]{:S(2)}) collective-permute-start(f32[1,16,128]{2,1,0:T(8,128)S(1)} %get-tuple-element.77), channel_id=1, source_target_pairs={{0,2},{2,4},{4,6},{1,3},{3,5},{5,7},{8,10},{10,12},{12,14},{9,11},... | collective-permute-start | bytes 24584 | tf_op jit(solution)/shard_map/ppermute | solution.py:21
  75.8 3.0 %collective-permute-start.20 = (f32[10,1,128]{2,1,0:T(1,128)S(1)}, f32[10,1,128]{2,1,0:T(1,128)S(1)}, u32[]{:S(2)}, u32[]{:S(2)}) collective-permute-start(f32[10,1,128]{2,1,0:T(1,128)S(1)} %get-tuple-element.51), channel_id=1, source_target_pairs={{0,1},{2,3},{4,5},{6,7},{8,9},{10,11},{12,13},{14,15},{16,17},{18,... | collective-permute-start | bytes 15368 | tf_op jit(solution)/shard_map/ppermute | solution.py:21
  81.2 5.7 %collective-permute-start.22 = (f32[1,16,128]{2,1,0:T(8,128)S(1)}, f32[1,16,128]{2,1,0:T(8,128)S(1)}, u32[]{:S(2)}, u32[]{:S(2)}) collective-permute-start(f32[1,16,128]{2,1,0:T(8,128)S(1)} %get-tuple-element.75), channel_id=1, source_target_pairs={{0,2},{2,4},{4,6},{1,3},{3,5},{5,7},{8,10},{10,12},{12,14},{9,11},... | collective-permute-start | bytes 24584 | tf_op jit(solution)/shard_map/ppermute | solution.py:21
  89.6 3.0 %collective-permute-start.24 = (f32[10,1,128]{2,1,0:T(1,128)S(1)}, f32[10,1,128]{2,1,0:T(1,128)S(1)}, u32[]{:S(2)}, u32[]{:S(2)}) collective-permute-start(f32[10,1,128]{2,1,0:T(1,128)S(1)} %get-tuple-element.49), channel_id=1, source_target_pairs={{0,1},{2,3},{4,5},{6,7},{8,9},{10,11},{12,13},{14,15},{16,17},{18,... | collective-permute-start | bytes 15368 | tf_op jit(solution)/shard_map/ppermute | solution.py:21
  95.1 5.7 %collective-permute-start.26 = (f32[1,16,128]{2,1,0:T(8,128)S(1)}, f32[1,16,128]{2,1,0:T(8,128)S(1)}, u32[]{:S(2)}, u32[]{:S(2)}) collective-permute-start(f32[1,16,128]{2,1,0:T(8,128)S(1)} %get-tuple-element.73), channel_id=1, source_target_pairs={{0,2},{2,4},{4,6},{1,3},{3,5},{5,7},{8,10},{10,12},{12,14},{9,11},... | collective-permute-start | bytes 24584 | tf_op jit(solution)/shard_map/ppermute | solution.py:21
  103.5 3.0 %collective-permute-start.28 = (f32[10,1,128]{2,1,0:T(1,128)S(1)}, f32[10,1,128]{2,1,0:T(1,128)S(1)}, u32[]{:S(2)}, u32[]{:S(2)}) collective-permute-start(f32[10,1,128]{2,1,0:T(1,128)S(1)} %get-tuple-element.47), channel_id=1, source_target_pairs={{0,1},{2,3},{4,5},{6,7},{8,9},{10,11},{12,13},{14,15},{16,17},{18,... | collective-permute-start | bytes 15368 | tf_op jit(solution)/shard_map/ppermute | solution.py:21
  108.9 5.7 %collective-permute-start.30 = (f32[1,16,128]{2,1,0:T(8,128)S(1)}, f32[1,16,128]{2,1,0:T(8,128)S(1)}, u32[]{:S(2)}, u32[]{:S(2)}) collective-permute-start(f32[1,16,128]{2,1,0:T(8,128)S(1)} %get-tuple-element.71), channel_id=1, source_target_pairs={{0,2},{2,4},{4,6},{1,3},{3,5},{5,7},{8,10},{10,12},{12,14},{9,11},... | collective-permute-start | bytes 24584 | tf_op jit(solution)/shard_map/ppermute | solution.py:21
  117.3 3.0 %collective-permute-start.32 = (f32[10,1,128]{2,1,0:T(1,128)S(1)}, f32[10,1,128]{2,1,0:T(1,128)S(1)}, u32[]{:S(2)}, u32[]{:S(2)}) collective-permute-start(f32[10,1,128]{2,1,0:T(1,128)S(1)} %get-tuple-element.45), channel_id=1, source_target_pairs={{0,1},{2,3},{4,5},{6,7},{8,9},{10,11},{12,13},{14,15},{16,17},{18,... | collective-permute-start | bytes 15368 | tf_op jit(solution)/shard_map/ppermute | solution.py:21
  121.4 18.6 %while.10 = (s32[]{:T(128)}, f32[8,16,128]{2,1,0:T(8,128)S(1)}, f32[8,16,128]{2,1,0:T(8,128)S(1)}, f32[8,16,128]{2,1,0:T(8,128)S(1)}, s32[]{:T(128)}) while((s32[]{:T(128)}, f32[8,16,128]{2,1,0:T(8,128)S(1)}, f32[8,16,128]{2,1,0:T(8,128)S(1)}, f32[8,16,128]{2,1,0:T(8,128)S(1)}, s32[]{:T(128)}) %tuple.50), condition=%wide.region_3.4_spmd, body=%wide.region_2.3_spmd.sunk | while | flops 32770 | bytes 524389 | solution.py:77
  122.7 4.9 %collective-permute-done = f32[8,16,128]{2,1,0:T(8,128)S(1)} collective-permute-done((f32[8,16,128]{2,1,0:T(8,128)S(1)}, f32[8,16,128]{2,1,0:T(8,128)S(1)}, u32[]{:S(2)}, u32[]{:S(2)}) %collective-permute-start) | collective-permute-done | bytes 65568 | tf_op jit(solution)/shard_map/while/body/eval_jaxpr/ppermute | solution.py:30
  129.0 4.9 %collective-permute-done = f32[8,16,128]{2,1,0:T(8,128)S(1)} collective-permute-done((f32[8,16,128]{2,1,0:T(8,128)S(1)}, f32[8,16,128]{2,1,0:T(8,128)S(1)}, u32[]{:S(2)}, u32[]{:S(2)}) %collective-permute-start) | collective-permute-done | bytes 65568 | tf_op jit(solution)/shard_map/while/body/eval_jaxpr/ppermute | solution.py:30
  135.2 4.9 %collective-permute-done = f32[8,16,128]{2,1,0:T(8,128)S(1)} collective-permute-done((f32[8,16,128]{2,1,0:T(8,128)S(1)}, f32[8,16,128]{2,1,0:T(8,128)S(1)}, u32[]{:S(2)}, u32[]{:S(2)}) %collective-permute-start) | collective-permute-done | bytes 65568 | tf_op jit(solution)/shard_map/while/body/eval_jaxpr/ppermute | solution.py:30
  141.4 4.9 %collective-permute-done.33 = f32[8,16,128]{2,1,0:T(8,128)S(1)} collective-permute-done((f32[8,16,128]{2,1,0:T(8,128)S(1)}, f32[8,16,128]{2,1,0:T(8,128)S(1)}, u32[]{:S(2)}, u32[]{:S(2)}) %collective-permute-start.33) | collective-permute-done | bytes 65568 | tf_op jit(solution)/shard_map/ppermute | solution.py:30
  147.6 5.7 %collective-permute-start.35 = (f32[1,16,128]{2,1,0:T(8,128)S(1)}, f32[1,16,128]{2,1,0:T(8,128)S(1)}, u32[]{:S(2)}, u32[]{:S(2)}) collective-permute-start(f32[1,16,128]{2,1,0:T(8,128)S(1)} %get-tuple-element.69), channel_id=1, source_target_pairs={{0,2},{2,4},{4,6},{1,3},{3,5},{5,7},{8,10},{10,12},{12,14},{9,11},... | collective-permute-start | bytes 24584 | tf_op jit(solution)/shard_map/ppermute | solution.py:21
  155.9 3.0 %collective-permute-start.37 = (f32[10,1,128]{2,1,0:T(1,128)S(1)}, f32[10,1,128]{2,1,0:T(1,128)S(1)}, u32[]{:S(2)}, u32[]{:S(2)}) collective-permute-start(f32[10,1,128]{2,1,0:T(1,128)S(1)} %get-tuple-element.43), channel_id=1, source_target_pairs={{0,1},{2,3},{4,5},{6,7},{8,9},{10,11},{12,13},{14,15},{16,17},{18,... | collective-permute-start | bytes 15368 | tf_op jit(solution)/shard_map/ppermute | solution.py:21
  161.4 5.7 %collective-permute-start.39 = (f32[1,16,128]{2,1,0:T(8,128)S(1)}, f32[1,16,128]{2,1,0:T(8,128)S(1)}, u32[]{:S(2)}, u32[]{:S(2)}) collective-permute-start(f32[1,16,128]{2,1,0:T(8,128)S(1)} %get-tuple-element.67), channel_id=1, source_target_pairs={{0,2},{2,4},{4,6},{1,3},{3,5},{5,7},{8,10},{10,12},{12,14},{9,11},... | collective-permute-start | bytes 24584 | tf_op jit(solution)/shard_map/ppermute | solution.py:21
  169.8 3.0 %collective-permute-start.41 = (f32[10,1,128]{2,1,0:T(1,128)S(1)}, f32[10,1,128]{2,1,0:T(1,128)S(1)}, u32[]{:S(2)}, u32[]{:S(2)}) collective-permute-start(f32[10,1,128]{2,1,0:T(1,128)S(1)} %get-tuple-element.41), channel_id=1, source_target_pairs={{0,1},{2,3},{4,5},{6,7},{8,9},{10,11},{12,13},{14,15},{16,17},{18,... | collective-permute-start | bytes 15368 | tf_op jit(solution)/shard_map/ppermute | solution.py:21
  175.2 5.7 %collective-permute-start.43 = (f32[1,16,128]{2,1,0:T(8,128)S(1)}, f32[1,16,128]{2,1,0:T(8,128)S(1)}, u32[]{:S(2)}, u32[]{:S(2)}) collective-permute-start(f32[1,16,128]{2,1,0:T(8,128)S(1)} %get-tuple-element.65), channel_id=1, source_target_pairs={{0,2},{2,4},{4,6},{1,3},{3,5},{5,7},{8,10},{10,12},{12,14},{9,11},... | collective-permute-start | bytes 24584 | tf_op jit(solution)/shard_map/ppermute | solution.py:21
  183.6 3.0 %collective-permute-start.45 = (f32[10,1,128]{2,1,0:T(1,128)S(1)}, f32[10,1,128]{2,1,0:T(1,128)S(1)}, u32[]{:S(2)}, u32[]{:S(2)}) collective-permute-start(f32[10,1,128]{2,1,0:T(1,128)S(1)} %get-tuple-element.39), channel_id=1, source_target_pairs={{0,1},{2,3},{4,5},{6,7},{8,9},{10,11},{12,13},{14,15},{16,17},{18,... | collective-permute-start | bytes 15368 | tf_op jit(solution)/shard_map/ppermute | solution.py:21
  189.0 5.7 %collective-permute-start.47 = (f32[1,16,128]{2,1,0:T(8,128)S(1)}, f32[1,16,128]{2,1,0:T(8,128)S(1)}, u32[]{:S(2)}, u32[]{:S(2)}) collective-permute-start(f32[1,16,128]{2,1,0:T(8,128)S(1)} %get-tuple-element.63), channel_id=1, source_target_pairs={{0,2},{2,4},{4,6},{1,3},{3,5},{5,7},{8,10},{10,12},{12,14},{9,11},... | collective-permute-start | bytes 24584 | tf_op jit(solution)/shard_map/ppermute | solution.py:21
  197.4 3.0 %collective-permute-start.49 = (f32[10,1,128]{2,1,0:T(1,128)S(1)}, f32[10,1,128]{2,1,0:T(1,128)S(1)}, u32[]{:S(2)}, u32[]{:S(2)}) collective-permute-start(f32[10,1,128]{2,1,0:T(1,128)S(1)} %get-tuple-element.37), channel_id=1, source_target_pairs={{0,1},{2,3},{4,5},{6,7},{8,9},{10,11},{12,13},{14,15},{16,17},{18,... | collective-permute-start | bytes 15368 | tf_op jit(solution)/shard_map/ppermute | solution.py:21
  203.7 37.4 %all-reduce.14.cloned.1.call-done = f32[8,16,128]{2,1,0:T(8,128)} async-done(((f32[8,16,128]{2,1,0:T(8,128)}), f32[8,16,128]{2,1,0:T(8,128)}) %all-reduce.14.cloned.1.call-update) | async-done | bytes 65552 | tf_op jit(solution)/shard_map/psum | solution.py:86
  241.1 1.5 neg.3
  (150 shorter events, 67.1 us)
Async XLA Ops:
  7.2 233.9 %all-reduce.14.cloned.1.call-start = ((), (), s32[]{:S(2)}) async-start(), calls=%async_computation | async-start | bytes 131072 | tf_op jit(solution)/shard_map/psum | solution.py:86
  7.3 6.8 %collective-permute-start.1 = (f32[1,16,128]{2,1,0:T(8,128)S(1)}, f32[1,16,128]{2,1,0:T(8,128)S(1)}, u32[]{:S(2)}, u32[]{:S(2)}) collective-permute-start(f32[1,16,128]{2,1,0:T(8,128)S(1)} %get-tuple-element.86), channel_id=1, source_target_pairs={{2,0},{4,2},{6,4},{3,1},{5,3},{7,5},{10,8},{12,10},{14,12},{11,9},... | collective-permute-start | bytes 24584 | tf_op jit(solution)/shard_map/ppermute | solution.py:22
  8.6 6.8 %collective-permute-start.2 = (f32[1,16,128]{2,1,0:T(8,128)S(1)}, f32[1,16,128]{2,1,0:T(8,128)S(1)}, u32[]{:S(2)}, u32[]{:S(2)}) collective-permute-start(f32[1,16,128]{2,1,0:T(8,128)S(1)} %get-tuple-element.85), channel_id=1, source_target_pairs={{0,2},{2,4},{4,6},{1,3},{3,5},{5,7},{8,10},{10,12},{12,14},{9,11},... | collective-permute-start | bytes 24584 | tf_op jit(solution)/shard_map/ppermute | solution.py:21
  15.4 5.4 %collective-permute-start.3 = (f32[10,1,128]{2,1,0:T(1,128)S(1)}, f32[10,1,128]{2,1,0:T(1,128)S(1)}, u32[]{:S(2)}, u32[]{:S(2)}) collective-permute-start(f32[10,1,128]{2,1,0:T(1,128)S(1)} %get-tuple-element.60), channel_id=1, source_target_pairs={{1,0},{3,2},{5,4},{7,6},{9,8},{11,10},{13,12},{15,14},{17,16},{19,... | collective-permute-start | bytes 15368 | tf_op jit(solution)/shard_map/ppermute | solution.py:22
  21.7 6.8 %collective-permute-start.5 = (f32[1,16,128]{2,1,0:T(8,128)S(1)}, f32[1,16,128]{2,1,0:T(8,128)S(1)}, u32[]{:S(2)}, u32[]{:S(2)}) collective-permute-start(f32[1,16,128]{2,1,0:T(8,128)S(1)} %get-tuple-element.84), channel_id=1, source_target_pairs={{2,0},{4,2},{6,4},{3,1},{5,3},{7,5},{10,8},{12,10},{14,12},{11,9},... | collective-permute-start | bytes 24584 | tf_op jit(solution)/shard_map/ppermute | solution.py:22
  23.0 6.8 %collective-permute-start.6 = (f32[1,16,128]{2,1,0:T(8,128)S(1)}, f32[1,16,128]{2,1,0:T(8,128)S(1)}, u32[]{:S(2)}, u32[]{:S(2)}) collective-permute-start(f32[1,16,128]{2,1,0:T(8,128)S(1)} %get-tuple-element.83), channel_id=1, source_target_pairs={{0,2},{2,4},{4,6},{1,3},{3,5},{5,7},{8,10},{10,12},{12,14},{9,11},... | collective-permute-start | bytes 24584 | tf_op jit(solution)/shard_map/ppermute | solution.py:21
  29.8 4.5 %collective-permute-start.7 = (f32[10,1,128]{2,1,0:T(1,128)S(1)}, f32[10,1,128]{2,1,0:T(1,128)S(1)}, u32[]{:S(2)}, u32[]{:S(2)}) collective-permute-start(f32[10,1,128]{2,1,0:T(1,128)S(1)} %get-tuple-element.58), channel_id=1, source_target_pairs={{1,0},{3,2},{5,4},{7,6},{9,8},{11,10},{13,12},{15,14},{17,16},{19,... | collective-permute-start | bytes 15368 | tf_op jit(solution)/shard_map/ppermute | solution.py:22
  35.4 6.4 %collective-permute-start.10 = (f32[1,16,128]{2,1,0:T(8,128)S(1)}, f32[1,16,128]{2,1,0:T(8,128)S(1)}, u32[]{:S(2)}, u32[]{:S(2)}) collective-permute-start(f32[1,16,128]{2,1,0:T(8,128)S(1)} %get-tuple-element.81), channel_id=1, source_target_pairs={{0,2},{2,4},{4,6},{1,3},{3,5},{5,7},{8,10},{10,12},{12,14},{9,11},... | collective-permute-start | bytes 24584 | tf_op jit(solution)/shard_map/ppermute | solution.py:21
  40.5 6.7 %collective-permute-start.9 = (f32[1,16,128]{2,1,0:T(8,128)S(1)}, f32[1,16,128]{2,1,0:T(8,128)S(1)}, u32[]{:S(2)}, u32[]{:S(2)}) collective-permute-start(f32[1,16,128]{2,1,0:T(8,128)S(1)} %get-tuple-element.82), channel_id=1, source_target_pairs={{2,0},{4,2},{6,4},{3,1},{5,3},{7,5},{10,8},{12,10},{14,12},{11,9},... | collective-permute-start | bytes 24584 | tf_op jit(solution)/shard_map/ppermute | solution.py:22
  52.7 6.8 %collective-permute-start.13 = (f32[1,16,128]{2,1,0:T(8,128)S(1)}, f32[1,16,128]{2,1,0:T(8,128)S(1)}, u32[]{:S(2)}, u32[]{:S(2)}) collective-permute-start(f32[1,16,128]{2,1,0:T(8,128)S(1)} %get-tuple-element.80), channel_id=1, source_target_pairs={{2,0},{4,2},{6,4},{3,1},{5,3},{7,5},{10,8},{12,10},{14,12},{11,9},... | collective-permute-start | bytes 24584 | tf_op jit(solution)/shard_map/ppermute | solution.py:22
  54.0 6.8 %collective-permute-start.14 = (f32[1,16,128]{2,1,0:T(8,128)S(1)}, f32[1,16,128]{2,1,0:T(8,128)S(1)}, u32[]{:S(2)}, u32[]{:S(2)}) collective-permute-start(f32[1,16,128]{2,1,0:T(8,128)S(1)} %get-tuple-element.79), channel_id=1, source_target_pairs={{0,2},{2,4},{4,6},{1,3},{3,5},{5,7},{8,10},{10,12},{12,14},{9,11},... | collective-permute-start | bytes 24584 | tf_op jit(solution)/shard_map/ppermute | solution.py:21
  66.4 6.8 %collective-permute-start.17 = (f32[1,16,128]{2,1,0:T(8,128)S(1)}, f32[1,16,128]{2,1,0:T(8,128)S(1)}, u32[]{:S(2)}, u32[]{:S(2)}) collective-permute-start(f32[1,16,128]{2,1,0:T(8,128)S(1)} %get-tuple-element.78), channel_id=1, source_target_pairs={{2,0},{4,2},{6,4},{3,1},{5,3},{7,5},{10,8},{12,10},{14,12},{11,9},... | collective-permute-start | bytes 24584 | tf_op jit(solution)/shard_map/ppermute | solution.py:22
  67.7 6.8 %collective-permute-start.18 = (f32[1,16,128]{2,1,0:T(8,128)S(1)}, f32[1,16,128]{2,1,0:T(8,128)S(1)}, u32[]{:S(2)}, u32[]{:S(2)}) collective-permute-start(f32[1,16,128]{2,1,0:T(8,128)S(1)} %get-tuple-element.77), channel_id=1, source_target_pairs={{0,2},{2,4},{4,6},{1,3},{3,5},{5,7},{8,10},{10,12},{12,14},{9,11},... | collective-permute-start | bytes 24584 | tf_op jit(solution)/shard_map/ppermute | solution.py:21
  74.5 4.5 %collective-permute-start.19 = (f32[10,1,128]{2,1,0:T(1,128)S(1)}, f32[10,1,128]{2,1,0:T(1,128)S(1)}, u32[]{:S(2)}, u32[]{:S(2)}) collective-permute-start(f32[10,1,128]{2,1,0:T(1,128)S(1)} %get-tuple-element.52), channel_id=1, source_target_pairs={{1,0},{3,2},{5,4},{7,6},{9,8},{11,10},{13,12},{15,14},{17,16},{19,... | collective-permute-start | bytes 15368 | tf_op jit(solution)/shard_map/ppermute | solution.py:22
  79.9 7.0 %collective-permute-start.21 = (f32[1,16,128]{2,1,0:T(8,128)S(1)}, f32[1,16,128]{2,1,0:T(8,128)S(1)}, u32[]{:S(2)}, u32[]{:S(2)}) collective-permute-start(f32[1,16,128]{2,1,0:T(8,128)S(1)} %get-tuple-element.76), channel_id=1, source_target_pairs={{2,0},{4,2},{6,4},{3,1},{5,3},{7,5},{10,8},{12,10},{14,12},{11,9},... | collective-permute-start | bytes 24584 | tf_op jit(solution)/shard_map/ppermute | solution.py:22
  81.2 7.1 %collective-permute-start.22 = (f32[1,16,128]{2,1,0:T(8,128)S(1)}, f32[1,16,128]{2,1,0:T(8,128)S(1)}, u32[]{:S(2)}, u32[]{:S(2)}) collective-permute-start(f32[1,16,128]{2,1,0:T(8,128)S(1)} %get-tuple-element.75), channel_id=1, source_target_pairs={{0,2},{2,4},{4,6},{1,3},{3,5},{5,7},{8,10},{10,12},{12,14},{9,11},... | collective-permute-start | bytes 24584 | tf_op jit(solution)/shard_map/ppermute | solution.py:21
  93.8 7.0 %collective-permute-start.25 = (f32[1,16,128]{2,1,0:T(8,128)S(1)}, f32[1,16,128]{2,1,0:T(8,128)S(1)}, u32[]{:S(2)}, u32[]{:S(2)}) collective-permute-start(f32[1,16,128]{2,1,0:T(8,128)S(1)} %get-tuple-element.74), channel_id=1, source_target_pairs={{2,0},{4,2},{6,4},{3,1},{5,3},{7,5},{10,8},{12,10},{14,12},{11,9},... | collective-permute-start | bytes 24584 | tf_op jit(solution)/shard_map/ppermute | solution.py:22
  95.1 7.1 %collective-permute-start.26 = (f32[1,16,128]{2,1,0:T(8,128)S(1)}, f32[1,16,128]{2,1,0:T(8,128)S(1)}, u32[]{:S(2)}, u32[]{:S(2)}) collective-permute-start(f32[1,16,128]{2,1,0:T(8,128)S(1)} %get-tuple-element.73), channel_id=1, source_target_pairs={{0,2},{2,4},{4,6},{1,3},{3,5},{5,7},{8,10},{10,12},{12,14},{9,11},... | collective-permute-start | bytes 24584 | tf_op jit(solution)/shard_map/ppermute | solution.py:21
  107.6 7.0 %collective-permute-start.29 = (f32[1,16,128]{2,1,0:T(8,128)S(1)}, f32[1,16,128]{2,1,0:T(8,128)S(1)}, u32[]{:S(2)}, u32[]{:S(2)}) collective-permute-start(f32[1,16,128]{2,1,0:T(8,128)S(1)} %get-tuple-element.72), channel_id=1, source_target_pairs={{2,0},{4,2},{6,4},{3,1},{5,3},{7,5},{10,8},{12,10},{14,12},{11,9},... | collective-permute-start | bytes 24584 | tf_op jit(solution)/shard_map/ppermute | solution.py:22
  108.9 7.1 %collective-permute-start.30 = (f32[1,16,128]{2,1,0:T(8,128)S(1)}, f32[1,16,128]{2,1,0:T(8,128)S(1)}, u32[]{:S(2)}, u32[]{:S(2)}) collective-permute-start(f32[1,16,128]{2,1,0:T(8,128)S(1)} %get-tuple-element.71), channel_id=1, source_target_pairs={{0,2},{2,4},{4,6},{1,3},{3,5},{5,7},{8,10},{10,12},{12,14},{9,11},... | collective-permute-start | bytes 24584 | tf_op jit(solution)/shard_map/ppermute | solution.py:21
  121.4 6.2 %collective-permute-start = (f32[8,16,128]{2,1,0:T(8,128)S(1)}, f32[8,16,128]{2,1,0:T(8,128)S(1)}, u32[]{:S(2)}, u32[]{:S(2)}) collective-permute-start(f32[8,16,128]{2,1,0:T(8,128)S(1)} %get-tuple-element.120), channel_id=1, source_target_pairs={{8,0},{16,8},{24,16},{9,1},{17,9},{25,17},{10,2},{18,10},{26,18},{... | collective-permute-start | bytes 196616 | tf_op jit(solution)/shard_map/while/body/eval_jaxpr/ppermute | solution.py:30
  127.7 6.2 %collective-permute-start = (f32[8,16,128]{2,1,0:T(8,128)S(1)}, f32[8,16,128]{2,1,0:T(8,128)S(1)}, u32[]{:S(2)}, u32[]{:S(2)}) collective-permute-start(f32[8,16,128]{2,1,0:T(8,128)S(1)} %get-tuple-element.120), channel_id=1, source_target_pairs={{8,0},{16,8},{24,16},{9,1},{17,9},{25,17},{10,2},{18,10},{26,18},{... | collective-permute-start | bytes 196616 | tf_op jit(solution)/shard_map/while/body/eval_jaxpr/ppermute | solution.py:30
  133.9 6.2 %collective-permute-start = (f32[8,16,128]{2,1,0:T(8,128)S(1)}, f32[8,16,128]{2,1,0:T(8,128)S(1)}, u32[]{:S(2)}, u32[]{:S(2)}) collective-permute-start(f32[8,16,128]{2,1,0:T(8,128)S(1)} %get-tuple-element.120), channel_id=1, source_target_pairs={{8,0},{16,8},{24,16},{9,1},{17,9},{25,17},{10,2},{18,10},{26,18},{... | collective-permute-start | bytes 196616 | tf_op jit(solution)/shard_map/while/body/eval_jaxpr/ppermute | solution.py:30
  140.1 6.2 %collective-permute-start.33 = (f32[8,16,128]{2,1,0:T(8,128)S(1)}, f32[8,16,128]{2,1,0:T(8,128)S(1)}, u32[]{:S(2)}, u32[]{:S(2)}) collective-permute-start(f32[8,16,128]{2,1,0:T(8,128)S(1)} %get-tuple-element.24), channel_id=1, source_target_pairs={{8,0},{16,8},{24,16},{9,1},{17,9},{25,17},{10,2},{18,10},{26,18},{... | collective-permute-start | bytes 196616 | tf_op jit(solution)/shard_map/ppermute | solution.py:30
  146.3 7.0 %collective-permute-start.34 = (f32[1,16,128]{2,1,0:T(8,128)S(1)}, f32[1,16,128]{2,1,0:T(8,128)S(1)}, u32[]{:S(2)}, u32[]{:S(2)}) collective-permute-start(f32[1,16,128]{2,1,0:T(8,128)S(1)} %get-tuple-element.70), channel_id=1, source_target_pairs={{2,0},{4,2},{6,4},{3,1},{5,3},{7,5},{10,8},{12,10},{14,12},{11,9},... | collective-permute-start | bytes 24584 | tf_op jit(solution)/shard_map/ppermute | solution.py:22
  147.6 7.1 %collective-permute-start.35 = (f32[1,16,128]{2,1,0:T(8,128)S(1)}, f32[1,16,128]{2,1,0:T(8,128)S(1)}, u32[]{:S(2)}, u32[]{:S(2)}) collective-permute-start(f32[1,16,128]{2,1,0:T(8,128)S(1)} %get-tuple-element.69), channel_id=1, source_target_pairs={{0,2},{2,4},{4,6},{1,3},{3,5},{5,7},{8,10},{10,12},{12,14},{9,11},... | collective-permute-start | bytes 24584 | tf_op jit(solution)/shard_map/ppermute | solution.py:21
  160.1 7.0 %collective-permute-start.38 = (f32[1,16,128]{2,1,0:T(8,128)S(1)}, f32[1,16,128]{2,1,0:T(8,128)S(1)}, u32[]{:S(2)}, u32[]{:S(2)}) collective-permute-start(f32[1,16,128]{2,1,0:T(8,128)S(1)} %get-tuple-element.68), channel_id=1, source_target_pairs={{2,0},{4,2},{6,4},{3,1},{5,3},{7,5},{10,8},{12,10},{14,12},{11,9},... | collective-permute-start | bytes 24584 | tf_op jit(solution)/shard_map/ppermute | solution.py:22
  161.4 7.1 %collective-permute-start.39 = (f32[1,16,128]{2,1,0:T(8,128)S(1)}, f32[1,16,128]{2,1,0:T(8,128)S(1)}, u32[]{:S(2)}, u32[]{:S(2)}) collective-permute-start(f32[1,16,128]{2,1,0:T(8,128)S(1)} %get-tuple-element.67), channel_id=1, source_target_pairs={{0,2},{2,4},{4,6},{1,3},{3,5},{5,7},{8,10},{10,12},{12,14},{9,11},... | collective-permute-start | bytes 24584 | tf_op jit(solution)/shard_map/ppermute | solution.py:21
  173.9 7.0 %collective-permute-start.42 = (f32[1,16,128]{2,1,0:T(8,128)S(1)}, f32[1,16,128]{2,1,0:T(8,128)S(1)}, u32[]{:S(2)}, u32[]{:S(2)}) collective-permute-start(f32[1,16,128]{2,1,0:T(8,128)S(1)} %get-tuple-element.66), channel_id=1, source_target_pairs={{2,0},{4,2},{6,4},{3,1},{5,3},{7,5},{10,8},{12,10},{14,12},{11,9},... | collective-permute-start | bytes 24584 | tf_op jit(solution)/shard_map/ppermute | solution.py:22
  175.2 7.1 %collective-permute-start.43 = (f32[1,16,128]{2,1,0:T(8,128)S(1)}, f32[1,16,128]{2,1,0:T(8,128)S(1)}, u32[]{:S(2)}, u32[]{:S(2)}) collective-permute-start(f32[1,16,128]{2,1,0:T(8,128)S(1)} %get-tuple-element.65), channel_id=1, source_target_pairs={{0,2},{2,4},{4,6},{1,3},{3,5},{5,7},{8,10},{10,12},{12,14},{9,11},... | collective-permute-start | bytes 24584 | tf_op jit(solution)/shard_map/ppermute | solution.py:21
  187.7 7.0 %collective-permute-start.46 = (f32[1,16,128]{2,1,0:T(8,128)S(1)}, f32[1,16,128]{2,1,0:T(8,128)S(1)}, u32[]{:S(2)}, u32[]{:S(2)}) collective-permute-start(f32[1,16,128]{2,1,0:T(8,128)S(1)} %get-tuple-element.64), channel_id=1, source_target_pairs={{2,0},{4,2},{6,4},{3,1},{5,3},{7,5},{10,8},{12,10},{14,12},{11,9},... | collective-permute-start | bytes 24584 | tf_op jit(solution)/shard_map/ppermute | solution.py:22
  189.0 7.1 %collective-permute-start.47 = (f32[1,16,128]{2,1,0:T(8,128)S(1)}, f32[1,16,128]{2,1,0:T(8,128)S(1)}, u32[]{:S(2)}, u32[]{:S(2)}) collective-permute-start(f32[1,16,128]{2,1,0:T(8,128)S(1)} %get-tuple-element.63), channel_id=1, source_target_pairs={{0,2},{2,4},{4,6},{1,3},{3,5},{5,7},{8,10},{10,12},{12,14},{9,11},... | collective-permute-start | bytes 24584 | tf_op jit(solution)/shard_map/ppermute | solution.py:21
  (27 other events, 103.3 us)
Sparse Core Ops, SparseCore 0:
  203.8 37.2 all-reduce.13
where the time goes:
time: 251 us; the launch traced here: 249 us
  starting transfers between devices  140 us (56%)
  waiting for transfers between devices  85.8 us (34%)
  between operations  15 us (6%)
  other arithmetic  6.44 us (3%)
    ppermute x24, starting transfers between devices, with_halo(): before = lax.ppermute(last, axis, up)  103 us
    psum x1, waiting for transfers between devices, shards(): damping_grad = -lax.psum(partial_grad, 'tm')  37.4 us
    ppermute x24, starting transfers between devices, with_halo(): after = lax.ppermute(leading, axis, down)  31 us
    ppermute x24, waiting for transfers between devices, with_halo(): before = lax.ppermute(last, axis, up)  23.4 us
    ppermute x4, waiting for transfers between devices, passed_along(): lax.ppermute(value, axis, [(source, source + steps) for source in range(l...  19.5 us
    ppermute x24, waiting for transfers between devices, with_halo(): after = lax.ppermute(leading, axis, down)  5.43 us
    ppermute x4, starting transfers between devices, passed_along(): lax.ppermute(value, axis, [(source, source + steps) for source in range(l...  5.17 us
  transfers between devices with their start and end apart: 53, of which 28 were waited for; matrix products, arithmetic and copies ran while one was open for 0% of the time, Pallas kernels for 0%

commit v1 on v0

v1 whole, which is shorter than its diff:
```python
import functools

import jax
import jax.numpy as jnp
from jax import lax
from jax.experimental import pallas as pl
from jax.experimental.pallas import tpu as pltpu
from jax.sharding import PartitionSpec as P

MESH = pl.DeviceIdType.MESH
SWEEPS = 4
BLOCK_CELLS = 8
COUPLING = 0.5
H = SWEEPS
HY = 8

XLO, XHI, YS, CLO, CHI, MAIN0, MAIN1 = range(7)


def kernel(
    nt, ns, src_ref, fs_ref, term_ref, damp_ref, stiff_ref, reg_ref,
    adj_ref, grad_ref,
    g, m, xa, xb, c, r, p, tot,
    g_send, g_recv, h_send, h_recv, u_send, m_send, m_recv, r_send, r_recv, t_send, t_recv,
):
    steps, bx, by, cz = src_ref.shape
    ex, ey = bx + 2 * H, by + HY
    t = lax.axis_index("tm")
    sx = lax.axis_index("sx")
    sy = lax.axis_index("sy")
    last = t == nt - 1
    other = 1 - sy
    has_lo, has_hi = sx > 0, sx < ns - 1
    always = t >= 0
    ys = pl.multiple_of(other * HY, HY)

    core = pl.ds(0, by)
    edge = pl.ds(ys, HY)
    far = pl.ds(by, HY)
    pieces = [
        (XHI, has_lo, sx - 1, sy, (0, H), H + bx, core, core),
        (XLO, has_hi, sx + 1, sy, (bx - H, bx), 0, core, core),
        (YS, always, sx, other, (0, bx), H, edge, far),
        (CHI, has_lo, sx - 1, other, (0, H - 1), H + bx, edge, far),
        (CLO, has_hi, sx + 1, other, (bx - H + 1, bx), 1, edge, far),
    ]
    arrives = {XLO: has_lo, XHI: has_hi, YS: always, CLO: has_lo, CHI: has_hi}

    zero = jnp.zeros((ex, ey, cz), jnp.float32)
    for field in range(3):
        g[field] = zero
    m[...] = zero

    barrier = pltpu.get_barrier_semaphore()

    def greet(cond, dev):
        @pl.when(cond)
        def _():
            pl.semaphore_signal(barrier, inc=1, device_id=dev, device_id_type=MESH)

    for slot, cond, dx, dy, *_ in pieces:
        greet(cond, (t, dx, dy))
    for dt, cond_t in ((t - 1, t > 0), (t + 1, t < nt - 1)):
        greet(cond_t, (dt, sx, sy))
        for slot, cond, dx, dy, *_ in pieces:
            greet(jnp.logical_and(cond_t, cond), (dt, dx, dy))
    greet(t >= 2, (0, sx, sy))
    for k in range(2, nt):
        greet(t == 0, (k, sx, sy))
    one = lambda cond: jnp.where(cond, 1, 0)
    around = 2 * (one(has_lo) + one(has_hi)) + 1
    slabs = one(t > 0) + one(t < nt - 1)
    friends = around + slabs * (around + 1) + one(t >= 2) + one(t == 0) * (nt - 2)

    def reaction(step):
        columns = []
        for j in range(by // BLOCK_CELLS):
            rows = slice(j * BLOCK_CELLS, (j + 1) * BLOCK_CELLS)
            parts = []
            for i in range(bx // BLOCK_CELLS):
                cells = slice(i * BLOCK_CELLS, (i + 1) * BLOCK_CELLS)
                parts.append(damp_ref[cells, rows, :] + stiff_ref[reg_ref[step, i, j]])
            columns.append(jnp.concatenate(parts, axis=0) if len(parts) > 1 else parts[0])
        return jnp.concatenate(columns, axis=1)

    react_lo, react_hi = reaction(0), reaction(1)
    inv_lo = 1.0 / (1.0 + react_lo + 6.0 * COUPLING)
    inv_hi = 1.0 / (1.0 + react_hi + 6.0 * COUPLING)
    factor = 1.0 / (1.0 + steps * react_lo)
    c[...] = factor
    body = pl.ds(H, bx)
    g[0, body, core, :] = jnp.where(last, term_ref[...], src_ref[1])
    g[1, body, core, :] = jnp.where(last, inv_hi, inv_lo)
    g[2, body, core, :] = jnp.where(last, inv_lo, inv_hi)

    def piece_copy(piece, src, off, dst, dt, send, recv, fields=None):
        slot, cond, dx, dy, (lo, hi), to, ysrc, ydst = piece
        s_at = (pl.ds(off + lo, hi - lo), ysrc)
        d_at = (pl.ds(to, hi - lo), ydst)
        if fields is not None:
            s_at, d_at = (fields,) + s_at, (fields,) + d_at
        return pltpu.make_async_remote_copy(
            src_ref=src.at[s_at], dst_ref=dst.at[d_at],
            send_sem=send.at[slot], recv_sem=recv.at[slot],
            device_id=(dt, dx, dy), device_id_type=MESH,
        )

    def start(cond, copy):
        @pl.when(cond)
        def _():
            copy.start()

    def wait_in(cond, copy):
        @pl.when(cond)
        def _():
            copy.wait_recv()

    def wait_out(cond, copy):
        @pl.when(cond)
        def _():
            copy.wait_send()

    first = [(q, piece_copy(q, g, H, g, t, g_send, g_recv, pl.ds(0, 2))) for q in pieces]
    second = [(q, piece_copy(q, g, H, g, t, h_send, h_recv, pl.ds(2, 1))) for q in pieces]
    around_m = [(q, piece_copy(q, m, H, m, t, u_send, m_recv)) for q in pieces]
    down = [(q, piece_copy(q, c, 0, m, t - 1, m_send, m_recv)) for q in pieces]
    half = bx // 2
    mains = [
        pltpu.make_async_remote_copy(
            src_ref=c.at[pl.ds(i * half, half)], dst_ref=m.at[pl.ds(H + i * half, half), core],
            send_sem=m_send.at[MAIN0 + i], recv_sem=m_recv.at[MAIN0 + i],
            device_id=(t - 1, sx, sy), device_id_type=MESH,
        )
        for i in range(2)
    ]

    pl.semaphore_wait(barrier, friends)
    for q, copy in first:
        start(q[1], copy)
    for q, copy in second:
        start(q[1], copy)

    lane = lax.broadcasted_iota(jnp.int32, (ey, cz), 1)
    row = lax.broadcasted_iota(jnp.int32, (ey, cz), 0)
    no_before = jnp.logical_and(row == 0, sy == 0)
    no_after = jnp.logical_and(row == by - 1, sy == 1)
    z_first, z_last = lane == 0, lane == cz - 1

    def phi(b, inv):
        bufs = [b, xa, xb]
        cur = b
        out = []
        for s in range(1, SWEEPS + 1):
            nxt = xa if s % 2 else xb
            for i in range(s, ex - s):
                x = cur[i]
                total = cur[i - 1] + cur[i + 1]
                total += jnp.where(no_before, 0.0, pltpu.roll(x, 1, 0))
                total += jnp.where(no_after, 0.0, pltpu.roll(x, ey - 1, 0))
                total += jnp.where(z_first, 0.0, pltpu.roll(x, 1, 1))
                total += jnp.where(z_last, 0.0, pltpu.roll(x, cz - 1, 1))
                value = (b[i] + COUPLING * total) * inv[i]
                if s == SWEEPS:
                    out.append(value[:by])
                else:
                    nxt[i] = value
            cur = nxt
        return out

    def arrived(copies):
        for q, copy in copies:
            wait_in(arrives[q[0]], copy)

    arrived(first)
    y1 = phi(g.at[0], g.at[1])
    arrived(second)

    @pl.when(last)
    def _():
        for i in range(bx):
            value = y1[i] + src_ref[1, i]
            adj_ref[1, i] = value
            m[H + i, core, :] = value
        for q, copy in around_m:
            start(q[1], copy)
        arrived(around_m)
        top = phi(m, g.at[2])
        for i in range(bx):
            c[i] = top[i] + src_ref[0, i]

    not_last = jnp.logical_not(last)

    @pl.when(not_last)
    def _():
        for i in range(bx):
            adj_ref[0, i] = y1[i] + src_ref[0, i]

    def send_half(i):
        start(t > 0, mains[i])
        for q, copy in down:
            if q[0] in ((XHI, CHI) if i == 0 else (XLO, CLO, YS)):
                start(jnp.logical_and(t > 0, q[1]), copy)

    for i in range(2):
        rows = pl.ds(i * half, half)

        @pl.when(not_last)
        def _():
            mains[i].wait_recv()
            c[rows] = c[rows] * m[pl.ds(H + i * half, half), core, :] + adj_ref[0, rows]

        send_half(i)
    adj_ref[0] = c[...]

    @pl.when(not_last)
    def _():
        arrived(down)
        top = phi(m, g.at[2])
        for i in range(bx):
            adj_ref[1, i] = top[i] + src_ref[1, i]

    p[...] = -(adj_ref[0] * fs_ref[0] + adj_ref[1] * fs_ref[1])
    to_prev = pltpu.make_async_remote_copy(
        src_ref=p, dst_ref=r, send_sem=r_send.at[0], recv_sem=r_recv.at[0],
        device_id=(t - 1, sx, sy), device_id_type=MESH,
    )
    spread = [
        pltpu.make_async_remote_copy(
            src_ref=p, dst_ref=tot, send_sem=t_send.at[k], recv_sem=t_recv.at[0],
            device_id=(k, sx, sy), device_id_type=MESH,
        )
        for k in range(1, nt)
    ]

    @pl.when(not_last)
    def _():
        to_prev.wait_recv()
        p[...] += r[...]

    @pl.when(t > 0)
    def _():
        to_prev.start()
        spread[0].wait_recv()
        grad_ref[...] = tot[...]
        to_prev.wait_send()
        for copy in mains:
            copy.wait_send()

    @pl.when(t == 0)
    def _():
        for copy in spread:
            copy.start()
        grad_ref[...] = p[...]
        for copy in spread:
            copy.wait_send()

    for q, copy in first + second:
        wait_out(q[1], copy)
    for q, copy in around_m:
        wait_out(jnp.logical_and(last, q[1]), copy)
    for q, copy in down:
        wait_out(jnp.logical_and(t > 0, q[1]), copy)


def shards(sources, forward_states, terminal, damping, contact_stiff, regions):
    nt, ns = lax.axis_size("tm"), lax.axis_size("sx")
    steps, bx, by, cz = sources.shape
    assert steps == 2 and lax.axis_size("sy") == 2
    vmem = pl.BlockSpec(memory_space=pltpu.VMEM)
    smem = pl.BlockSpec(memory_space=pltpu.SMEM)
    f32 = jnp.float32
    ext = (bx + 2 * H, by + HY, cz)
    block = (bx, by, cz)
    dma = pltpu.SemaphoreType.DMA
    return pl.pallas_call(
        functools.partial(kernel, nt, ns),
        out_shape=(
            jax.ShapeDtypeStruct(sources.shape, f32),
            jax.ShapeDtypeStruct(block, f32),
        ),
        in_specs=[vmem] * 4 + [smem] * 2,
        out_specs=(vmem, vmem),
        scratch_shapes=[
            pltpu.VMEM((3,) + ext, f32),
            pltpu.VMEM(ext, f32),
            pltpu.VMEM(ext, f32),
            pltpu.VMEM(ext, f32),
            pltpu.VMEM(block, f32),
            pltpu.VMEM(block, f32),
            pltpu.VMEM(block, f32),
            pltpu.VMEM(block, f32),
            dma((5,)), dma((5,)), dma((5,)), dma((5,)), dma((5,)),
            dma((7,)), dma((7,)), dma((1,)), dma((1,)), dma((nt,)), dma((1,)),
        ],
        compiler_params=pltpu.CompilerParams(
            collective_id=0, has_side_effects=True, vmem_limit_bytes=32 * 1024 * 1024
        ),
    )(sources, forward_states, terminal, damping, contact_stiff, regions)


def solution(mesh):
    in_specs = (
        P("tm", "sx", "sy", None),
        P("tm", "sx", "sy", None),
        P("sx", "sy", None),
        P("sx", "sy", None),
        P(),
        P("tm", "sx", "sy"),
    )
    out_specs = (P("tm", "sx", "sy", None), P("sx", "sy", None))
    return jax.shard_map(shards, mesh=mesh, in_specs=in_specs, out_specs=out_specs, check_vma=False)
```

time: 251 us -> 41.8 us (0.17)
  the two profiles are of different devices: /device:TPU:0 before, /device:TPU:28 now
where the time goes in v1:
time: 41.8 us; the launch traced here: 41.6 us
  Pallas kernels  34.8 us (83%)
  local copies, waits for them, and re-layouts  6.1 us (15%)
  between operations  0.65 us (2%)
    pallas_call x1, Pallas kernels, shards(): pl.pallas_call(functools.partial(kernel, nt, ns), out_shape=(jax.ShapeDty...  34.8 us
    unnamed x14, local copies, waits for them, and re-layouts  6.1 us

profile of v1, /device:TPU:28, one launch (start us, length us, event | category | flops | bytes accessed | tf_op | source)
XLA Modules:
  0.0 41.6 jit_solution(15934739301810349306)
XLA Ops:
  0.6 0.0 copy-start
  0.6 0.9 %copy-done = f32[2,8,16,128]{3,2,1,0:T(8,128)S(1)} copy-done((f32[2,8,16,128]{3,2,1,0:T(8,128)S(1)}, f32[2,8,16,128]{3,2,1,0:T(8,128)}, u32[]{:S(2)}) %copy-start) | copy-done | bytes 131096
  1.5 0.0 copy-start.1
  1.5 0.9 %copy-done.1 = f32[2,8,16,128]{3,2,1,0:T(8,128)S(1)} copy-done((f32[2,8,16,128]{3,2,1,0:T(8,128)S(1)}, f32[2,8,16,128]{3,2,1,0:T(8,128)}, u32[]{:S(2)}) %copy-start.1) | copy-done | bytes 131096
  2.4 0.0 copy-start.2
  2.4 0.8 %copy-done.2 = f32[8,16,128]{2,1,0:T(8,128)S(1)} copy-done((f32[8,16,128]{2,1,0:T(8,128)S(1)}, f32[8,16,128]{2,1,0:T(8,128)}, u32[]{:S(2)}) %copy-start.2) | copy-done | bytes 65560
  3.3 0.0 copy-start.3
  3.3 0.8 %copy-done.3 = f32[8,16,128]{2,1,0:T(8,128)S(1)} copy-done((f32[8,16,128]{2,1,0:T(8,128)S(1)}, f32[8,16,128]{2,1,0:T(8,128)}, u32[]{:S(2)}) %copy-start.3) | copy-done | bytes 65560
  4.1 0.0 copy-start.4
  4.1 0.7 %copy-done.4 = s32[2,1,2]{2,1,0:T(1,128)S(1)} copy-done((s32[2,1,2]{2,1,0:T(1,128)S(1)}, s32[2,1,2]{2,1,0:T(1,128)}, u32[]{:S(2)}) %copy-start.4) | copy-done | bytes 40
  4.8 0.0 copy-start.5
  4.8 0.7 %copy-done.5 = f32[8]{0:T(128)S(1)} copy-done((f32[8]{0:T(128)S(1)}, f32[8]{0:T(128)}, u32[]{:S(2)}) %copy-start.5) | copy-done | bytes 56
  5.5 34.8 %shard_map.77 = (f32[2,8,16,128]{3,2,1,0:T(8,128)S(1)}, f32[8,16,128]{2,1,0:T(8,128)S(1)}) custom-call(f32[2,8,16,128]{3,2,1,0:T(8,128)S(1)} %copy-done, f32[2,8,16,128]{3,2,1,0:T(8,128)S(1)} %copy-done.1, f32[8,16,128]{2,1,0:T(8,128)S(1)} %copy-done.2, f32[8,16,128]{2,1,0:T(8,128)S(1)} %copy-done.3, f32[8]{0:T(128)S(1)} %copy-done.5, s32[2,1,2]{2,1,0:T(1,128)S(1)} %copy-done.4), custom_call_target="tpu_custom_call" | custom-call | tf_op jit(solution)/shard_map/pallas_call | solution.py:275
  40.3 0.7 %copy.10 = f32[2,8,16,128]{3,2,1,0:T(8,128)} copy(f32[2,8,16,128]{3,2,1,0:T(8,128)S(1)} %get-tuple-element.4) | data formatting | bytes 262144
  40.9 0.6 %copy.11 = f32[8,16,128]{2,1,0:T(8,128)} copy(f32[8,16,128]{2,1,0:T(8,128)S(1)} %get-tuple-element.5) | data formatting | bytes 131072
Async XLA Ops:
  0.6 0.9 %copy-start = (f32[2,8,16,128]{3,2,1,0:T(8,128)S(1)}, f32[2,8,16,128]{3,2,1,0:T(8,128)}, u32[]{:S(2)}) copy-start(f32[2,8,16,128]{3,2,1,0:T(8,128)} %src_ref.1) | copy-start | bytes 393220
  1.5 0.9 %copy-start.1 = (f32[2,8,16,128]{3,2,1,0:T(8,128)S(1)}, f32[2,8,16,128]{3,2,1,0:T(8,128)}, u32[]{:S(2)}) copy-start(f32[2,8,16,128]{3,2,1,0:T(8,128)} %fs_ref.1) | copy-start | bytes 393220
  2.4 0.8 %copy-start.2 = (f32[8,16,128]{2,1,0:T(8,128)S(1)}, f32[8,16,128]{2,1,0:T(8,128)}, u32[]{:S(2)}) copy-start(f32[8,16,128]{2,1,0:T(8,128)} %term_ref.1) | copy-start | bytes 196612
  3.3 0.8 %copy-start.3 = (f32[8,16,128]{2,1,0:T(8,128)S(1)}, f32[8,16,128]{2,1,0:T(8,128)}, u32[]{:S(2)}) copy-start(f32[8,16,128]{2,1,0:T(8,128)} %damp_ref.1) | copy-start | bytes 196612
  4.1 0.7 %copy-start.4 = (s32[2,1,2]{2,1,0:T(1,128)S(1)}, s32[2,1,2]{2,1,0:T(1,128)}, u32[]{:S(2)}) copy-start(s32[2,1,2]{2,1,0:T(1,128)} %reg_ref.1) | copy-start | bytes 52
  4.8 0.7 %copy-start.5 = (f32[8]{0:T(128)S(1)}, f32[8]{0:T(128)}, u32[]{:S(2)}) copy-start(f32[8]{0:T(128)} %stiff_ref.1) | copy-start | bytes 100

commit v2 on v1

--- a/solution.py
+++ b/solution.py
@@ -18,10 +18,11 @@
 
 
 def kernel(
-    nt, ns, src_ref, fs_ref, term_ref, damp_ref, stiff_ref, reg_ref,
+    nt, ns, src_hbm, fs_hbm, term_hbm, damp_hbm, stiff_hbm, reg_hbm,
     adj_ref, grad_ref,
+    src_ref, fs_ref, stiff_ref, reg_ref, picks, inv,
     g, m, xa, xb, c, r, p, tot,
-    g_send, g_recv, h_send, h_recv, u_send, m_send, m_recv, r_send, r_recv, t_send, t_recv,
+    l_sem, g_send, g_recv, h_send, h_recv, u_send, m_send, m_recv, r_send, r_recv, t_send, t_recv,
 ):
     steps, bx, by, cz = src_ref.shape
     ex, ey = bx + 2 * H, by + HY
@@ -46,10 +47,37 @@
     ]
     arrives = {XLO: has_lo, XHI: has_hi, YS: always, CLO: has_lo, CHI: has_hi}
 
-    zero = jnp.zeros((ex, ey, cz), jnp.float32)
-    for field in range(3):
-        g[field] = zero
-    m[...] = zero
+    body = pl.ds(H, bx)
+    own = g.at[0, body, core]
+    loads = [
+        pltpu.make_async_copy(stiff_hbm, stiff_ref, l_sem.at[0]),
+        pltpu.make_async_copy(reg_hbm, reg_ref, l_sem.at[1]),
+        pltpu.make_async_copy(damp_hbm, g.at[1, body, core], l_sem.at[2]),
+        pltpu.make_async_copy(src_hbm, src_ref, l_sem.at[3]),
+        pltpu.make_async_copy(fs_hbm, fs_ref, l_sem.at[4]),
+    ]
+    from_term = pltpu.make_async_copy(term_hbm, own, l_sem.at[5])
+    from_src = pltpu.make_async_copy(src_hbm.at[1], own, l_sem.at[5])
+    for load in loads[:3]:
+        load.start()
+
+    @pl.when(t == nt - 1)
+    def _():
+        from_term.start()
+
+    @pl.when(t != nt - 1)
+    def _():
+        from_src.start()
+
+    for load in loads[3:]:
+        load.start()
+
+    edge_zero = jnp.zeros((H, ey, cz), jnp.float32)
+    far_zero = jnp.zeros((bx, HY, cz), jnp.float32)
+    for ref in (g.at[0], g.at[1], m):
+        ref[0:H] = edge_zero
+        ref[H + bx : ex] = edge_zero
+        ref[H : H + bx, by:ey] = far_zero
 
     barrier = pltpu.get_barrier_semaphore()
 
@@ -72,26 +100,14 @@
     slabs = one(t > 0) + one(t < nt - 1)
     friends = around + slabs * (around + 1) + one(t >= 2) + one(t == 0) * (nt - 2)
 
-    def reaction(step):
-        columns = []
-        for j in range(by // BLOCK_CELLS):
-            rows = slice(j * BLOCK_CELLS, (j + 1) * BLOCK_CELLS)
-            parts = []
-            for i in range(bx // BLOCK_CELLS):
-                cells = slice(i * BLOCK_CELLS, (i + 1) * BLOCK_CELLS)
-                parts.append(damp_ref[cells, rows, :] + stiff_ref[reg_ref[step, i, j]])
-            columns.append(jnp.concatenate(parts, axis=0) if len(parts) > 1 else parts[0])
-        return jnp.concatenate(columns, axis=1)
-
-    react_lo, react_hi = reaction(0), reaction(1)
-    inv_lo = 1.0 / (1.0 + react_lo + 6.0 * COUPLING)
-    inv_hi = 1.0 / (1.0 + react_hi + 6.0 * COUPLING)
-    factor = 1.0 / (1.0 + steps * react_lo)
-    c[...] = factor
-    body = pl.ds(H, bx)
-    g[0, body, core, :] = jnp.where(last, term_ref[...], src_ref[1])
-    g[1, body, core, :] = jnp.where(last, inv_hi, inv_lo)
-    g[2, body, core, :] = jnp.where(last, inv_lo, inv_hi)
+    blocks = by // BLOCK_CELLS
+    for load in loads[:2]:
+        load.wait()
+    late = jnp.where(t == nt - 1, 1, 0)
+    for j in range(blocks):
+        for k, step in enumerate((late, 1 - late)):
+            value = stiff_ref[reg_ref[step, 0, j]]
+            picks[5, j * steps + k : j * steps + k + 1, :] = jnp.full((1, cz), value, jnp.float32)
 
     def piece_copy(piece, src, off, dst, dt, send, recv, fields=None):
         slot, cond, dx, dy, (lo, hi), to, ysrc, ydst = piece
@@ -121,23 +137,36 @@
             copy.wait_send()
 
     first = [(q, piece_copy(q, g, H, g, t, g_send, g_recv, pl.ds(0, 2))) for q in pieces]
-    second = [(q, piece_copy(q, g, H, g, t, h_send, h_recv, pl.ds(2, 1))) for q in pieces]
+    second = [
+        (
+            q,
+            pltpu.make_async_remote_copy(
+                src_ref=picks.at[5], dst_ref=picks.at[q[0]],
+                send_sem=h_send.at[q[0]], recv_sem=h_recv.at[q[0]],
+                device_id=(t, q[2], q[3]), device_id_type=MESH,
+            ),
+        )
+        for q in pieces
+    ]
     around_m = [(q, piece_copy(q, m, H, m, t, u_send, m_recv)) for q in pieces]
     down = [(q, piece_copy(q, c, 0, m, t - 1, m_send, m_recv)) for q in pieces]
-    half = bx // 2
+    chunks = 4
+    half = bx // chunks
     mains = [
         pltpu.make_async_remote_copy(
             src_ref=c.at[pl.ds(i * half, half)], dst_ref=m.at[pl.ds(H + i * half, half), core],
             send_sem=m_send.at[MAIN0 + i], recv_sem=m_recv.at[MAIN0 + i],
             device_id=(t - 1, sx, sy), device_id_type=MESH,
         )
-        for i in range(2)
+        for i in range(chunks)
     ]
 
     pl.semaphore_wait(barrier, friends)
+    for q, copy in second:
+        start(q[1], copy)
+    loads[2].wait()
+    from_src.wait()
     for q, copy in first:
-        start(q[1], copy)
-    for q, copy in second:
         start(q[1], copy)
 
     lane = lax.broadcasted_iota(jnp.int32, (ey, cz), 1)
@@ -171,9 +200,33 @@
         for q, copy in copies:
             wait_in(arrives[q[0]], copy)
 
+    def pick(slot, j, k):
+        return picks[slot, j * steps + k : j * steps + k + 1, :]
+
+    def near_pick(slot, k):
+        if blocks == 1:
+            return pick(slot, 0, k)
+        return jnp.where(sy == 1, pick(slot, blocks - 1, k), pick(slot, 0, k))
+
+    def fill(out, k, rows, straight, corner, inside):
+        for i in rows:
+            for j in range(blocks):
+                cells = slice(j * BLOCK_CELLS, (j + 1) * BLOCK_CELLS)
+                value = 1.0 / (1.0 + (pick(straight, j, k) + g[1, i, cells, :]) + 6.0 * COUPLING)
+                inv[out, i, cells, :] = jnp.where(inside, value, 0.0)
+            value = 1.0 / (1.0 + (near_pick(corner, k) + g[1, i, by:ey, :]) + 6.0 * COUPLING)
+            inv[out, i, by:ey, :] = jnp.where(inside, value, 0.0)
+
+    def fill_all(out, k):
+        fill(out, k, range(1, H), XLO, CLO, has_lo)
+        fill(out, k, range(H, H + bx), 5, YS, always)
+        fill(out, k, range(H + bx, ex - 1), XHI, CHI, has_hi)
+
+    loads[3].wait()
+    arrived(second)
     arrived(first)
-    y1 = phi(g.at[0], g.at[1])
-    arrived(second)
+    fill_all(0, 0)
+    y1 = phi(g.at[0], inv.at[0])
 
     @pl.when(last)
     def _():
@@ -183,8 +236,13 @@
             m[H + i, core, :] = value
         for q, copy in around_m:
             start(q[1], copy)
+
+    fill_all(1, 1)
+
+    @pl.when(last)
+    def _():
         arrived(around_m)
-        top = phi(m, g.at[2])
+        top = phi(m, inv.at[1])
         for i in range(bx):
             c[i] = top[i] + src_ref[0, i]
 
@@ -192,16 +250,13 @@
 
     @pl.when(not_last)
     def _():
+        for j in range(blocks):
+            cells = slice(j * BLOCK_CELLS, (j + 1) * BLOCK_CELLS)
+            c[:, cells, :] = 1.0 / (1.0 + steps * (pick(5, j, 0) + g[1, H : H + bx, cells, :]))
         for i in range(bx):
             adj_ref[0, i] = y1[i] + src_ref[0, i]
 
-    def send_half(i):
-        start(t > 0, mains[i])
-        for q, copy in down:
-            if q[0] in ((XHI, CHI) if i == 0 else (XLO, CLO, YS)):
-                start(jnp.logical_and(t > 0, q[1]), copy)
-
-    for i in range(2):
+    for i in range(chunks):
         rows = pl.ds(i * half, half)
 
         @pl.when(not_last)
@@ -209,16 +264,19 @@
             mains[i].wait_recv()
             c[rows] = c[rows] * m[pl.ds(H + i * half, half), core, :] + adj_ref[0, rows]
 
-        send_half(i)
+        start(t > 0, mains[i])
+    for q, copy in down:
+        start(jnp.logical_and(t > 0, q[1]), copy)
     adj_ref[0] = c[...]
 
     @pl.when(not_last)
     def _():
         arrived(down)
-        top = phi(m, g.at[2])
+        top = phi(m, inv.at[1])
         for i in range(bx):
             adj_ref[1, i] = top[i] + src_ref[1, i]
 
+    loads[4].wait()
     p[...] = -(adj_ref[0] * fs_ref[0] + adj_ref[1] * fs_ref[1])
     to_prev = pltpu.make_async_remote_copy(
         src_ref=p, dst_ref=r, send_sem=r_send.at[0], recv_sem=r_recv.at[0],
@@ -265,9 +323,9 @@
 def shards(sources, forward_states, terminal, damping, contact_stiff, regions):
     nt, ns = lax.axis_size("tm"), lax.axis_size("sx")
     steps, bx, by, cz = sources.shape
-    assert steps == 2 and lax.axis_size("sy") == 2
+    assert steps == 2 and bx == BLOCK_CELLS and lax.axis_size("sy") == 2
     vmem = pl.BlockSpec(memory_space=pltpu.VMEM)
-    smem = pl.BlockSpec(memory_space=pltpu.SMEM)
+    hbm = pl.BlockSpec(memory_space=pltpu.HBM)
     f32 = jnp.float32
     ext = (bx + 2 * H, by + HY, cz)
     block = (bx, by, cz)
@@ -278,10 +336,16 @@
             jax.ShapeDtypeStruct(sources.shape, f32),
             jax.ShapeDtypeStruct(block, f32),
         ),
-        in_specs=[vmem] * 4 + [smem] * 2,
+        in_specs=[hbm] * 6,
         out_specs=(vmem, vmem),
         scratch_shapes=[
-            pltpu.VMEM((3,) + ext, f32),
+            pltpu.VMEM(sources.shape, f32),
+            pltpu.VMEM(sources.shape, f32),
+            pltpu.SMEM(contact_stiff.shape, f32),
+            pltpu.SMEM(regions.shape, jnp.int32),
+            pltpu.VMEM((6, 8, cz), f32),
+            pltpu.VMEM((2,) + ext, f32),
+            pltpu.VMEM((2,) + ext, f32),
             pltpu.VMEM(ext, f32),
             pltpu.VMEM(ext, f32),
             pltpu.VMEM(ext, f32),
@@ -289,11 +353,11 @@
             pltpu.VMEM(block, f32),
             pltpu.VMEM(block, f32),
             pltpu.VMEM(block, f32),
-            dma((5,)), dma((5,)), dma((5,)), dma((5,)), dma((5,)),
-            dma((7,)), dma((7,)), dma((1,)), dma((1,)), dma((nt,)), dma((1,)),
+            dma((6,)), dma((5,)), dma((5,)), dma((5,)), dma((5,)), dma((5,)),
+            dma((9,)), dma((9,)), dma((1,)), dma((1,)), dma((nt,)), dma((1,)),
         ],
         compiler_params=pltpu.CompilerParams(
-            collective_id=0, has_side_effects=True, vmem_limit_bytes=32 * 1024 * 1024
+            collective_id=0, has_side_effects=True, vmem_limit_bytes=64 * 1024 * 1024
         ),
     )(sources, forward_states, terminal, damping, contact_stiff, regions)
 

time: 41.8 us -> 37.6 us (0.90)
  the two profiles are of different devices: /device:TPU:28 before, /device:TPU:0 now
where the time goes in v2:
time: 37.6 us; the launch traced here: 37.4 us
  Pallas kernels  34.5 us (92%)
  local copies, waits for them, and re-layouts  2.23 us (6%)
  between operations  0.65 us (2%)
    pallas_call x1, Pallas kernels, shards(): pl.pallas_call(functools.partial(kernel, nt, ns), out_shape=(jax.ShapeDty...  34.5 us
    unnamed x4, local copies, waits for them, and re-layouts  2.23 us

profile of v2, /device:TPU:0, one launch (start us, length us, event | category | flops | bytes accessed | tf_op | source)
XLA Modules:
  0.0 37.4 jit_solution(5906637397033473353)
XLA Ops:
  0.6 34.5 %shard_map.77 = (f32[2,8,16,128]{3,2,1,0:T(8,128)}, f32[8,16,128]{2,1,0:T(8,128)}) custom-call(f32[2,8,16,128]{3,2,1,0:T(8,128)} %src_hbm.1, f32[2,8,16,128]{3,2,1,0:T(8,128)} %fs_hbm.1, f32[8,16,128]{2,1,0:T(8,128)} %term_hbm.1, f32[8,16,128]{2,1,0:T(8,128)} %damp_hbm.1, f32[8]{0:T(128)} %stiff_hbm.1, s32[2,1,2]{2,1,0:T(1,128)} %reg_hbm.1), custom_call_target="tpu_custom_call" | custom-call | tf_op jit(solution)/shard_map/pallas_call | solution.py:333
  35.2 0.0 copy-start
  35.2 1.6 %copy.10 = f32[2,8,16,128]{3,2,1,0:T(8,128)} copy(f32[2,8,16,128]{3,2,1,0:T(8,128)} %get-tuple-element.4) | data formatting | bytes 262144
  36.8 0.0 copy-done
  36.8 0.6 %copy.11 = f32[8,16,128]{2,1,0:T(8,128)} copy(f32[8,16,128]{2,1,0:T(8,128)S(1)} %copy-done) | data formatting | bytes 131072
Async XLA Ops:
  35.2 1.6 %copy-start = (f32[8,16,128]{2,1,0:T(8,128)S(1)}, f32[8,16,128]{2,1,0:T(8,128)}, u32[]{:S(2)}) copy-start(f32[8,16,128]{2,1,0:T(8,128)} %get-tuple-element.5) | copy-start | bytes 196612

commit v3 on v2

--- a/solution.py
+++ b/solution.py
@@ -26,6 +26,8 @@
 ):
     steps, bx, by, cz = src_ref.shape
     ex, ey = bx + 2 * H, by + HY
+    parts = min(nt, bx)
+    size = bx // parts
     t = lax.axis_index("tm")
     sx = lax.axis_index("sx")
     sy = lax.axis_index("sy")
@@ -89,16 +91,14 @@
     for slot, cond, dx, dy, *_ in pieces:
         greet(cond, (t, dx, dy))
     for dt, cond_t in ((t - 1, t > 0), (t + 1, t < nt - 1)):
-        greet(cond_t, (dt, sx, sy))
         for slot, cond, dx, dy, *_ in pieces:
             greet(jnp.logical_and(cond_t, cond), (dt, dx, dy))
-    greet(t >= 2, (0, sx, sy))
-    for k in range(2, nt):
-        greet(t == 0, (k, sx, sy))
+    for k in range(nt):
+        greet(t != k, (k, sx, sy))
     one = lambda cond: jnp.where(cond, 1, 0)
     around = 2 * (one(has_lo) + one(has_hi)) + 1
     slabs = one(t > 0) + one(t < nt - 1)
-    friends = around + slabs * (around + 1) + one(t >= 2) + one(t == 0) * (nt - 2)
+    friends = around + slabs * around + nt - 1
 
     blocks = by // BLOCK_CELLS
     for load in loads[:2]:
@@ -278,38 +278,59 @@
 
     loads[4].wait()
     p[...] = -(adj_ref[0] * fs_ref[0] + adj_ref[1] * fs_ref[1])
-    to_prev = pltpu.make_async_remote_copy(
-        src_ref=p, dst_ref=r, send_sem=r_send.at[0], recv_sem=r_recv.at[0],
-        device_id=(t - 1, sx, sy), device_id_type=MESH,
-    )
-    spread = [
-        pltpu.make_async_remote_copy(
-            src_ref=p, dst_ref=tot, send_sem=t_send.at[k], recv_sem=t_recv.at[0],
-            device_id=(k, sx, sy), device_id_type=MESH,
-        )
-        for k in range(1, nt)
-    ]
-
-    @pl.when(not_last)
-    def _():
-        to_prev.wait_recv()
-        p[...] += r[...]
+
+    def part(q):
+        return pl.ds(q * size, size)
+
+    def gather_copy(q):
+        return pltpu.make_async_remote_copy(
+            src_ref=p.at[part(q)], dst_ref=r.at[t], send_sem=r_send.at[q], recv_sem=r_recv.at[t],
+            device_id=(q, sx, sy), device_id_type=MESH,
+        )
+
+    def arrival(k):
+        return pltpu.make_async_remote_copy(
+            src_ref=p.at[part(0)], dst_ref=r.at[k], send_sem=r_send.at[0], recv_sem=r_recv.at[k],
+            device_id=(0, sx, sy), device_id_type=MESH,
+        )
+
+    def spread_copy(q, k):
+        return pltpu.make_async_remote_copy(
+            src_ref=tot.at[part(q)], dst_ref=tot.at[part(q)], send_sem=t_send.at[k],
+            recv_sem=t_recv.at[q], device_id=(k, sx, sy), device_id_type=MESH,
+        )
+
+    for q in range(parts):
+        start(t != q, gather_copy(q))
+    for q in range(parts):
+
+        @pl.when(t == q)
+        def _():
+            total = p[part(q)]
+            for k in range(nt):
+                if k != q:
+                    arrival(k).wait_recv()
+                    total += r[k]
+            tot[part(q)] = total
+            for k in range(nt):
+                if k != q:
+                    spread_copy(q, k).start()
+
+    for q in range(parts):
+        wait_in(t != q, spread_copy(q, 0))
+    grad_ref[...] = tot[...]
+    for q in range(parts):
+        wait_out(t != q, gather_copy(q))
+
+        @pl.when(t == q)
+        def _():
+            for k in range(nt):
+                if k != q:
+                    spread_copy(q, k).wait_send()
 
     @pl.when(t > 0)
     def _():
-        to_prev.start()
-        spread[0].wait_recv()
-        grad_ref[...] = tot[...]
-        to_prev.wait_send()
         for copy in mains:
-            copy.wait_send()
-
-    @pl.when(t == 0)
-    def _():
-        for copy in spread:
-            copy.start()
-        grad_ref[...] = p[...]
-        for copy in spread:
             copy.wait_send()
 
     for q, copy in first + second:
@@ -350,11 +371,11 @@
             pltpu.VMEM(ext, f32),
             pltpu.VMEM(ext, f32),
             pltpu.VMEM(block, f32),
-            pltpu.VMEM(block, f32),
+            pltpu.VMEM((nt, bx // min(nt, bx), by, cz), f32),
             pltpu.VMEM(block, f32),
             pltpu.VMEM(block, f32),
             dma((6,)), dma((5,)), dma((5,)), dma((5,)), dma((5,)), dma((5,)),
-            dma((9,)), dma((9,)), dma((1,)), dma((1,)), dma((nt,)), dma((1,)),
+            dma((9,)), dma((9,)), dma((nt,)), dma((nt,)), dma((nt,)), dma((nt,)),
         ],
         compiler_params=pltpu.CompilerParams(
             collective_id=0, has_side_effects=True, vmem_limit_bytes=64 * 1024 * 1024

time: 37.6 us -> 40.2 us (1.069)
  Pallas kernels: 34.5 us -> 37.2 us
    pallas_call x1, Pallas kernels: 34.5 us -> 37.2 us  [shards(): pl.pallas_call(functools.partial(kernel, nt, ns), out_shape=(jax.ShapeDty...]
where the time goes in v3:
time: 40.2 us; the launch traced here: 40.1 us
  Pallas kernels  37.2 us (93%)
  local copies, waits for them, and re-layouts  2.23 us (6%)
  between operations  0.65 us (2%)
    pallas_call x1, Pallas kernels, shards(): pl.pallas_call(functools.partial(kernel, nt, ns), out_shape=(jax.ShapeDty...  37.2 us
    unnamed x4, local copies, waits for them, and re-layouts  2.23 us

profile of v3, /device:TPU:0, one launch (start us, length us, event | category | flops | bytes accessed | tf_op | source)
XLA Modules:
  0.0 40.1 jit_solution(9616996365511412141)
XLA Ops:
  0.6 37.2 %shard_map.77 = (f32[2,8,16,128]{3,2,1,0:T(8,128)}, f32[8,16,128]{2,1,0:T(8,128)}) custom-call(f32[2,8,16,128]{3,2,1,0:T(8,128)} %src_hbm.1, f32[2,8,16,128]{3,2,1,0:T(8,128)} %fs_hbm.1, f32[8,16,128]{2,1,0:T(8,128)} %term_hbm.1, f32[8,16,128]{2,1,0:T(8,128)} %damp_hbm.1, f32[8]{0:T(128)} %stiff_hbm.1, s32[2,1,2]{2,1,0:T(1,128)} %reg_hbm.1), custom_call_target="tpu_custom_call" | custom-call | tf_op jit(solution)/shard_map/pallas_call | solution.py:354
  37.8 0.0 copy-start
  37.8 1.6 %copy.10 = f32[2,8,16,128]{3,2,1,0:T(8,128)} copy(f32[2,8,16,128]{3,2,1,0:T(8,128)} %get-tuple-element.4) | data formatting | bytes 262144
  39.4 0.0 copy-done
  39.4 0.6 %copy.11 = f32[8,16,128]{2,1,0:T(8,128)} copy(f32[8,16,128]{2,1,0:T(8,128)S(1)} %copy-done) | data formatting | bytes 131072
Async XLA Ops:
  37.8 1.6 %copy-start = (f32[8,16,128]{2,1,0:T(8,128)S(1)}, f32[8,16,128]{2,1,0:T(8,128)}, u32[]{:S(2)}) copy-start(f32[8,16,128]{2,1,0:T(8,128)} %get-tuple-element.5) | copy-start | bytes 196612

commit v4 on v2

--- a/solution.py
+++ b/solution.py
@@ -19,10 +19,10 @@
 
 def kernel(
     nt, ns, src_hbm, fs_hbm, term_hbm, damp_hbm, stiff_hbm, reg_hbm,
-    adj_ref, grad_ref,
-    src_ref, fs_ref, stiff_ref, reg_ref, picks, inv,
+    adj_hbm, grad_hbm,
+    adj_ref, grad_ref, src_ref, fs_ref, stiff_ref, reg_ref, picks, inv,
     g, m, xa, xb, c, r, p, tot,
-    l_sem, g_send, g_recv, h_send, h_recv, u_send, m_send, m_recv, r_send, r_recv, t_send, t_recv,
+    l_sem, o_sem, g_send, g_recv, h_send, h_recv, u_send, m_send, m_recv, r_send, r_recv, t_send, t_recv,
 ):
     steps, bx, by, cz = src_ref.shape
     ex, ey = bx + 2 * H, by + HY
@@ -92,13 +92,15 @@
         greet(cond_t, (dt, sx, sy))
         for slot, cond, dx, dy, *_ in pieces:
             greet(jnp.logical_and(cond_t, cond), (dt, dx, dy))
-    greet(t >= 2, (0, sx, sy))
-    for k in range(2, nt):
-        greet(t == 0, (k, sx, sy))
+    for owner in range(2):
+        greet(t > owner + 1, (owner, sx, sy))
+        for k in range(owner + 2, nt):
+            greet(t == owner, (k, sx, sy))
     one = lambda cond: jnp.where(cond, 1, 0)
     around = 2 * (one(has_lo) + one(has_hi)) + 1
     slabs = one(t > 0) + one(t < nt - 1)
-    friends = around + slabs * (around + 1) + one(t >= 2) + one(t == 0) * (nt - 2)
+    friends = around + slabs * (around + 1) + one(t > 1) + one(t > 2)
+    friends += one(t == 0) * (nt - 2) + one(t == 1) * (nt - 3)
 
     blocks = by // BLOCK_CELLS
     for load in loads[:2]:
@@ -268,6 +270,12 @@
     for q, copy in down:
         start(jnp.logical_and(t > 0, q[1]), copy)
     adj_ref[0] = c[...]
+    saves = [
+        pltpu.make_async_copy(adj_ref.at[k], adj_hbm.at[k], o_sem.at[k]) for k in range(steps)
+    ]
+    saves[0].start()
+    loads[4].wait()
+    p[...] = c[...] * fs_ref[0]
 
     @pl.when(not_last)
     def _():
@@ -276,40 +284,58 @@
         for i in range(bx):
             adj_ref[1, i] = top[i] + src_ref[1, i]
 
-    loads[4].wait()
-    p[...] = -(adj_ref[0] * fs_ref[0] + adj_ref[1] * fs_ref[1])
+    p[...] = -(p[...] + adj_ref[1] * fs_ref[1])
     to_prev = pltpu.make_async_remote_copy(
         src_ref=p, dst_ref=r, send_sem=r_send.at[0], recv_sem=r_recv.at[0],
         device_id=(t - 1, sx, sy), device_id_type=MESH,
     )
-    spread = [
-        pltpu.make_async_remote_copy(
-            src_ref=p, dst_ref=tot, send_sem=t_send.at[k], recv_sem=t_recv.at[0],
+
+    def spread(owner, k):
+        return pltpu.make_async_remote_copy(
+            src_ref=p, dst_ref=tot.at[owner], send_sem=t_send.at[k], recv_sem=t_recv.at[owner],
             device_id=(k, sx, sy), device_id_type=MESH,
         )
-        for k in range(1, nt)
-    ]
-
-    @pl.when(not_last)
+
+    @pl.when(jnp.logical_and(not_last, t > 0))
     def _():
         to_prev.wait_recv()
         p[...] += r[...]
 
+    @pl.when(t >= 2)
+    def _():
+        to_prev.start()
+
+    for owner in range(2):
+
+        @pl.when(t == owner)
+        def _():
+            for k in range(nt - 1, -1, -1):
+                if k != owner:
+                    spread(owner, k).start()
+            tot[owner] = p[...]
+
+    saves[1].start()
+    for owner in range(2):
+        wait_in(t != owner, spread(owner, 0))
+    grad_ref[...] = tot[0] + tot[1]
+    save_grad = pltpu.make_async_copy(grad_ref, grad_hbm, o_sem.at[2])
+    save_grad.start()
+
+    @pl.when(t >= 2)
+    def _():
+        to_prev.wait_send()
+
+    for owner in range(2):
+
+        @pl.when(t == owner)
+        def _():
+            for k in range(nt):
+                if k != owner:
+                    spread(owner, k).wait_send()
+
     @pl.when(t > 0)
     def _():
-        to_prev.start()
-        spread[0].wait_recv()
-        grad_ref[...] = tot[...]
-        to_prev.wait_send()
         for copy in mains:
-            copy.wait_send()
-
-    @pl.when(t == 0)
-    def _():
-        for copy in spread:
-            copy.start()
-        grad_ref[...] = p[...]
-        for copy in spread:
             copy.wait_send()
 
     for q, copy in first + second:
@@ -318,13 +344,15 @@
         wait_out(jnp.logical_and(last, q[1]), copy)
     for q, copy in down:
         wait_out(jnp.logical_and(t > 0, q[1]), copy)
+    for save in saves:
+        save.wait()
+    save_grad.wait()
 
 
 def shards(sources, forward_states, terminal, damping, contact_stiff, regions):
     nt, ns = lax.axis_size("tm"), lax.axis_size("sx")
     steps, bx, by, cz = sources.shape
-    assert steps == 2 and bx == BLOCK_CELLS and lax.axis_size("sy") == 2
-    vmem = pl.BlockSpec(memory_space=pltpu.VMEM)
+    assert nt > 2 and steps == 2 and bx == BLOCK_CELLS and lax.axis_size("sy") == 2
     hbm = pl.BlockSpec(memory_space=pltpu.HBM)
     f32 = jnp.float32
     ext = (bx + 2 * H, by + HY, cz)
@@ -337,8 +365,10 @@
             jax.ShapeDtypeStruct(block, f32),
         ),
         in_specs=[hbm] * 6,
-        out_specs=(vmem, vmem),
+        out_specs=(hbm, hbm),
         scratch_shapes=[
+            pltpu.VMEM(sources.shape, f32),
+            pltpu.VMEM(block, f32),
             pltpu.VMEM(sources.shape, f32),
             pltpu.VMEM(sources.shape, f32),
             pltpu.SMEM(contact_stiff.shape, f32),
@@ -352,9 +382,9 @@
             pltpu.VMEM(block, f32),
             pltpu.VMEM(block, f32),
             pltpu.VMEM(block, f32),
-            pltpu.VMEM(block, f32),
-            dma((6,)), dma((5,)), dma((5,)), dma((5,)), dma((5,)), dma((5,)),
-            dma((9,)), dma((9,)), dma((1,)), dma((1,)), dma((nt,)), dma((1,)),
+            pltpu.VMEM((2,) + block, f32),
+            dma((6,)), dma((3,)), dma((5,)), dma((5,)), dma((5,)), dma((5,)), dma((5,)),
+            dma((9,)), dma((9,)), dma((1,)), dma((1,)), dma((nt,)), dma((2,)),
         ],
         compiler_params=pltpu.CompilerParams(
             collective_id=0, has_side_effects=True, vmem_limit_bytes=64 * 1024 * 1024

time: 37.6 us -> 36.4 us (0.968); the launches traced: 37.4 us -> 35.7 us
  Pallas kernels: 34.5 us -> 32.9 us
    pallas_call x1, Pallas kernels: 34.5 us -> 32.9 us  [shards(): pl.pallas_call(functools.partial(kernel, nt, ns), out_shape=(jax.ShapeDty...]
where the time goes in v4:
time: 36.4 us; the launch traced here: 35.7 us
  Pallas kernels  32.9 us (90%)
  local copies, waits for them, and re-layouts  2.23 us (6%)
  between operations  0.65 us (2%)
    pallas_call x1, Pallas kernels, shards(): pl.pallas_call(functools.partial(kernel, nt, ns), out_shape=(jax.ShapeDty...  32.9 us
    unnamed x4, local copies, waits for them, and re-layouts  2.23 us

profile of v4, /device:TPU:0, one launch (start us, length us, event | category | flops | bytes accessed | tf_op | source)
XLA Modules:
  0.0 35.7 jit_solution(4401928300303490067)
XLA Ops:
  0.6 32.9 %shard_map.77 = (f32[2,8,16,128]{3,2,1,0:T(8,128)}, f32[8,16,128]{2,1,0:T(8,128)}) custom-call(f32[2,8,16,128]{3,2,1,0:T(8,128)} %src_hbm.1, f32[2,8,16,128]{3,2,1,0:T(8,128)} %fs_hbm.1, f32[8,16,128]{2,1,0:T(8,128)} %term_hbm.1, f32[8,16,128]{2,1,0:T(8,128)} %damp_hbm.1, f32[8]{0:T(128)} %stiff_hbm.1, s32[2,1,2]{2,1,0:T(1,128)} %reg_hbm.1), custom_call_target="tpu_custom_call" | custom-call | tf_op jit(solution)/shard_map/pallas_call | solution.py:361
  33.5 0.0 copy-start
  33.5 1.6 %copy.10 = f32[2,8,16,128]{3,2,1,0:T(8,128)} copy(f32[2,8,16,128]{3,2,1,0:T(8,128)} %get-tuple-element.4) | data formatting | bytes 262144
  35.1 0.0 copy-done
  35.1 0.6 %copy.11 = f32[8,16,128]{2,1,0:T(8,128)} copy(f32[8,16,128]{2,1,0:T(8,128)S(1)} %copy-done) | data formatting | bytes 131072
Async XLA Ops:
  33.5 1.6 %copy-start = (f32[8,16,128]{2,1,0:T(8,128)S(1)}, f32[8,16,128]{2,1,0:T(8,128)}, u32[]{:S(2)}) copy-start(f32[8,16,128]{2,1,0:T(8,128)} %get-tuple-element.5) | copy-start | bytes 196612

commit v5 on v4

--- a/solution.py
+++ b/solution.py
@@ -22,7 +22,7 @@
     adj_hbm, grad_hbm,
     adj_ref, grad_ref, src_ref, fs_ref, stiff_ref, reg_ref, picks, inv,
     g, m, xa, xb, c, r, p, tot,
-    l_sem, o_sem, g_send, g_recv, h_send, h_recv, u_send, m_send, m_recv, r_send, r_recv, t_send, t_recv,
+    l_sem, o_sem, d_send, d_recv, g_send, g_recv, h_send, h_recv, u_send, m_send, m_recv, r_send, r_recv, t_send, t_recv,
 ):
     steps, bx, by, cz = src_ref.shape
     ex, ey = bx + 2 * H, by + HY
@@ -105,7 +105,7 @@
     blocks = by // BLOCK_CELLS
     for load in loads[:2]:
         load.wait()
-    late = jnp.where(t == nt - 1, 1, 0)
+    late = jnp.where(last, 1, 0)
     for j in range(blocks):
         for k, step in enumerate((late, 1 - late)):
             value = stiff_ref[reg_ref[step, 0, j]]
@@ -139,6 +139,8 @@
             copy.wait_send()
 
     first = [(q, piece_copy(q, g, H, g, t, g_send, g_recv, pl.ds(0, 2))) for q in pieces]
+    alone = [(q, piece_copy(q, g, H, g, t, g_send, g_recv, pl.ds(0, 1))) for q in pieces]
+    up = [(q, piece_copy(q, g, H, g, t + 1, d_send, d_recv, pl.ds(1, 1))) for q in pieces]
     second = [
         (
             q,
@@ -164,11 +166,26 @@
     ]
 
     pl.semaphore_wait(barrier, friends)
+    loads[2].wait()
+
+    @pl.when(t == nt - 2)
+    def _():
+        for q, copy in up:
+            start(q[1], copy)
+
+    from_src.wait()
+
+    @pl.when(last)
+    def _():
+        for q, copy in alone:
+            start(q[1], copy)
+
+    @pl.when(jnp.logical_not(last))
+    def _():
+        for q, copy in first:
+            start(q[1], copy)
+
     for q, copy in second:
-        start(q[1], copy)
-    loads[2].wait()
-    from_src.wait()
-    for q, copy in first:
         start(q[1], copy)
 
     lane = lax.broadcasted_iota(jnp.int32, (ey, cz), 1)
@@ -210,24 +227,45 @@
             return pick(slot, 0, k)
         return jnp.where(sy == 1, pick(slot, blocks - 1, k), pick(slot, 0, k))
 
-    def fill(out, k, rows, straight, corner, inside):
-        for i in rows:
+    def inverse(at, i, cells):
+        return 1.0 / (1.0 + (at + g[1, i, cells, :]) + 6.0 * COUPLING)
+
+    def fill_own(out):
+        for i in range(H, H + bx):
             for j in range(blocks):
                 cells = slice(j * BLOCK_CELLS, (j + 1) * BLOCK_CELLS)
-                value = 1.0 / (1.0 + (pick(straight, j, k) + g[1, i, cells, :]) + 6.0 * COUPLING)
-                inv[out, i, cells, :] = jnp.where(inside, value, 0.0)
-            value = 1.0 / (1.0 + (near_pick(corner, k) + g[1, i, by:ey, :]) + 6.0 * COUPLING)
-            inv[out, i, by:ey, :] = jnp.where(inside, value, 0.0)
-
-    def fill_all(out, k):
-        fill(out, k, range(1, H), XLO, CLO, has_lo)
-        fill(out, k, range(H, H + bx), 5, YS, always)
-        fill(out, k, range(H + bx, ex - 1), XHI, CHI, has_hi)
-
+                inv[out, i, cells, :] = inverse(pick(5, j, out), i, cells)
+
+    def fill_halo(out):
+        for rows, straight, corner, inside in (
+            (range(1, H), XLO, CLO, has_lo),
+            (range(H + bx, ex - 1), XHI, CHI, has_hi),
+        ):
+            for i in rows:
+                for j in range(blocks):
+                    cells = slice(j * BLOCK_CELLS, (j + 1) * BLOCK_CELLS)
+                    value = inverse(pick(straight, j, out), i, cells)
+                    inv[out, i, cells, :] = jnp.where(inside, value, 0.0)
+                value = inverse(near_pick(corner, out), i, slice(by, ey))
+                inv[out, i, by:ey, :] = jnp.where(inside, value, 0.0)
+        for i in range(H, H + bx):
+            inv[out, i, by:ey, :] = inverse(near_pick(YS, out), i, slice(by, ey))
+
+    fill_own(0)
+    fill_own(1)
     loads[3].wait()
     arrived(second)
-    arrived(first)
-    fill_all(0, 0)
+
+    @pl.when(last)
+    def _():
+        arrived(up)
+        arrived(alone)
+
+    @pl.when(jnp.logical_not(last))
+    def _():
+        arrived(first)
+
+    fill_halo(0)
     y1 = phi(g.at[0], inv.at[0])
 
     @pl.when(last)
@@ -239,7 +277,7 @@
         for q, copy in around_m:
             start(q[1], copy)
 
-    fill_all(1, 1)
+    fill_halo(1)
 
     @pl.when(last)
     def _():
@@ -338,7 +376,22 @@
         for copy in mains:
             copy.wait_send()
 
-    for q, copy in first + second:
+    @pl.when(last)
+    def _():
+        for q, copy in alone:
+            wait_out(q[1], copy)
+
+    @pl.when(not_last)
+    def _():
+        for q, copy in first:
+            wait_out(q[1], copy)
+
+    @pl.when(t == nt - 2)
+    def _():
+        for q, copy in up:
+            wait_out(q[1], copy)
+
+    for q, copy in second:
         wait_out(q[1], copy)
     for q, copy in around_m:
         wait_out(jnp.logical_and(last, q[1]), copy)
@@ -383,7 +436,7 @@
             pltpu.VMEM(block, f32),
             pltpu.VMEM(block, f32),
             pltpu.VMEM((2,) + block, f32),
-            dma((6,)), dma((3,)), dma((5,)), dma((5,)), dma((5,)), dma((5,)), dma((5,)),
+            dma((6,)), dma((3,)), dma((5,)), dma((5,)), dma((5,)), dma((5,)), dma((5,)), dma((5,)), dma((5,)),
             dma((9,)), dma((9,)), dma((1,)), dma((1,)), dma((nt,)), dma((2,)),
         ],
         compiler_params=pltpu.CompilerParams(

time: 36.4 us -> 36.8 us (1.011)
  Pallas kernels: 32.9 us -> 33.3 us
    pallas_call x1, Pallas kernels: 32.9 us -> 33.3 us  [shards(): pl.pallas_call(functools.partial(kernel, nt, ns), out_shape=(jax.ShapeDty...]
where the time goes in v5:
time: 36.8 us; the launch traced here: 36.1 us
  Pallas kernels  33.3 us (90%)
  local copies, waits for them, and re-layouts  2.23 us (6%)
  between operations  0.65 us (2%)
    pallas_call x1, Pallas kernels, shards(): pl.pallas_call(functools.partial(kernel, nt, ns), out_shape=(jax.ShapeDty...  33.3 us
    unnamed x4, local copies, waits for them, and re-layouts  2.23 us

profile of v5, /device:TPU:0, one launch (start us, length us, event | category | flops | bytes accessed | tf_op | source)
XLA Modules:
  0.0 36.1 jit_solution(2458425875206663359)
XLA Ops:
  0.6 33.3 %shard_map.77 = (f32[2,8,16,128]{3,2,1,0:T(8,128)}, f32[8,16,128]{2,1,0:T(8,128)}) custom-call(f32[2,8,16,128]{3,2,1,0:T(8,128)} %src_hbm.1, f32[2,8,16,128]{3,2,1,0:T(8,128)} %fs_hbm.1, f32[8,16,128]{2,1,0:T(8,128)} %term_hbm.1, f32[8,16,128]{2,1,0:T(8,128)} %damp_hbm.1, f32[8]{0:T(128)} %stiff_hbm.1, s32[2,1,2]{2,1,0:T(1,128)} %reg_hbm.1), custom_call_target="tpu_custom_call" | custom-call | tf_op jit(solution)/shard_map/pallas_call | solution.py:414
  33.9 0.0 copy-start
  33.9 1.6 %copy.10 = f32[2,8,16,128]{3,2,1,0:T(8,128)} copy(f32[2,8,16,128]{3,2,1,0:T(8,128)} %get-tuple-element.4) | data formatting | bytes 262144
  35.5 0.0 copy-done
  35.5 0.6 %copy.11 = f32[8,16,128]{2,1,0:T(8,128)} copy(f32[8,16,128]{2,1,0:T(8,128)S(1)} %copy-done) | data formatting | bytes 131072
Async XLA Ops:
  33.9 1.6 %copy-start = (f32[8,16,128]{2,1,0:T(8,128)S(1)}, f32[8,16,128]{2,1,0:T(8,128)}, u32[]{:S(2)}) copy-start(f32[8,16,128]{2,1,0:T(8,128)} %get-tuple-element.5) | copy-start | bytes 196612

commit v6 on v5

--- a/solution.py
+++ b/solution.py
@@ -22,7 +22,7 @@
     adj_hbm, grad_hbm,
     adj_ref, grad_ref, src_ref, fs_ref, stiff_ref, reg_ref, picks, inv,
     g, m, xa, xb, c, r, p, tot,
-    l_sem, o_sem, d_send, d_recv, g_send, g_recv, h_send, h_recv, u_send, m_send, m_recv, r_send, r_recv, t_send, t_recv,
+    l_sem, o_sem, g_send, g_recv, h_send, h_recv, u_send, m_send, m_recv, r_send, r_recv, t_send, t_recv,
 ):
     steps, bx, by, cz = src_ref.shape
     ex, ey = bx + 2 * H, by + HY
@@ -139,8 +139,6 @@
             copy.wait_send()
 
     first = [(q, piece_copy(q, g, H, g, t, g_send, g_recv, pl.ds(0, 2))) for q in pieces]
-    alone = [(q, piece_copy(q, g, H, g, t, g_send, g_recv, pl.ds(0, 1))) for q in pieces]
-    up = [(q, piece_copy(q, g, H, g, t + 1, d_send, d_recv, pl.ds(1, 1))) for q in pieces]
     second = [
         (
             q,
@@ -168,23 +166,9 @@
     pl.semaphore_wait(barrier, friends)
     loads[2].wait()
 
-    @pl.when(t == nt - 2)
-    def _():
-        for q, copy in up:
-            start(q[1], copy)
-
     from_src.wait()
-
-    @pl.when(last)
-    def _():
-        for q, copy in alone:
-            start(q[1], copy)
-
-    @pl.when(jnp.logical_not(last))
-    def _():
-        for q, copy in first:
-            start(q[1], copy)
-
+    for q, copy in first:
+        start(q[1], copy)
     for q, copy in second:
         start(q[1], copy)
 
@@ -255,16 +239,7 @@
     fill_own(1)
     loads[3].wait()
     arrived(second)
-
-    @pl.when(last)
-    def _():
-        arrived(up)
-        arrived(alone)
-
-    @pl.when(jnp.logical_not(last))
-    def _():
-        arrived(first)
-
+    arrived(first)
     fill_halo(0)
     y1 = phi(g.at[0], inv.at[0])
 
@@ -353,16 +328,29 @@
             tot[owner] = p[...]
 
     saves[1].start()
+    for q, copy in first + second:
+        wait_out(q[1], copy)
+    for q, copy in around_m:
+        wait_out(jnp.logical_and(last, q[1]), copy)
+
+    @pl.when(t > 0)
+    def _():
+        for copy in mains:
+            copy.wait_send()
+        for q, copy in down:
+            wait_out(q[1], copy)
+
+    @pl.when(t >= 2)
+    def _():
+        to_prev.wait_send()
+
+    saves[0].wait()
     for owner in range(2):
         wait_in(t != owner, spread(owner, 0))
     grad_ref[...] = tot[0] + tot[1]
     save_grad = pltpu.make_async_copy(grad_ref, grad_hbm, o_sem.at[2])
     save_grad.start()
 
-    @pl.when(t >= 2)
-    def _():
-        to_prev.wait_send()
-
     for owner in range(2):
 
         @pl.when(t == owner)
@@ -371,34 +359,7 @@
                 if k != owner:
                     spread(owner, k).wait_send()
 
-    @pl.when(t > 0)
-    def _():
-        for copy in mains:
-            copy.wait_send()
-
-    @pl.when(last)
-    def _():
-        for q, copy in alone:
-            wait_out(q[1], copy)
-
-    @pl.when(not_last)
-    def _():
-        for q, copy in first:
-            wait_out(q[1], copy)
-
-    @pl.when(t == nt - 2)
-    def _():
-        for q, copy in up:
-            wait_out(q[1], copy)
-
-    for q, copy in second:
-        wait_out(q[1], copy)
-    for q, copy in around_m:
-        wait_out(jnp.logical_and(last, q[1]), copy)
-    for q, copy in down:
-        wait_out(jnp.logical_and(t > 0, q[1]), copy)
-    for save in saves:
-        save.wait()
+    saves[1].wait()
     save_grad.wait()
 
 
@@ -436,7 +397,7 @@
             pltpu.VMEM(block, f32),
             pltpu.VMEM(block, f32),
             pltpu.VMEM((2,) + block, f32),
-            dma((6,)), dma((3,)), dma((5,)), dma((5,)), dma((5,)), dma((5,)), dma((5,)), dma((5,)), dma((5,)),
+            dma((6,)), dma((3,)), dma((5,)), dma((5,)), dma((5,)), dma((5,)), dma((5,)),
             dma((9,)), dma((9,)), dma((1,)), dma((1,)), dma((nt,)), dma((2,)),
         ],
         compiler_params=pltpu.CompilerParams(

time: 36.8 us -> 36.7 us (level)
  no operation moved by 1% of the time
where the time goes in v6:
time: 36.7 us; the launch traced here: 36 us
  Pallas kernels  33.2 us (90%)
  local copies, waits for them, and re-layouts  2.23 us (6%)
  between operations  0.65 us (2%)
    pallas_call x1, Pallas kernels, shards(): pl.pallas_call(functools.partial(kernel, nt, ns), out_shape=(jax.ShapeDty...  33.2 us
    unnamed x4, local copies, waits for them, and re-layouts  2.23 us

profile of v6, /device:TPU:0, one launch (start us, length us, event | category | flops | bytes accessed | tf_op | source)
XLA Modules:
  0.0 36.0 jit_solution(3565155111166125060)
XLA Ops:
  0.6 33.2 %shard_map.77 = (f32[2,8,16,128]{3,2,1,0:T(8,128)}, f32[8,16,128]{2,1,0:T(8,128)}) custom-call(f32[2,8,16,128]{3,2,1,0:T(8,128)} %src_hbm.1, f32[2,8,16,128]{3,2,1,0:T(8,128)} %fs_hbm.1, f32[8,16,128]{2,1,0:T(8,128)} %term_hbm.1, f32[8,16,128]{2,1,0:T(8,128)} %damp_hbm.1, f32[8]{0:T(128)} %stiff_hbm.1, s32[2,1,2]{2,1,0:T(1,128)} %reg_hbm.1), custom_call_target="tpu_custom_call" | custom-call | tf_op jit(solution)/shard_map/pallas_call | solution.py:375
  33.8 0.0 copy-start
  33.8 1.6 %copy.10 = f32[2,8,16,128]{3,2,1,0:T(8,128)} copy(f32[2,8,16,128]{3,2,1,0:T(8,128)} %get-tuple-element.4) | data formatting | bytes 262144
  35.4 0.0 copy-done
  35.4 0.6 %copy.11 = f32[8,16,128]{2,1,0:T(8,128)} copy(f32[8,16,128]{2,1,0:T(8,128)S(1)} %copy-done) | data formatting | bytes 131072
Async XLA Ops:
  33.8 1.6 %copy-start = (f32[8,16,128]{2,1,0:T(8,128)S(1)}, f32[8,16,128]{2,1,0:T(8,128)}, u32[]{:S(2)}) copy-start(f32[8,16,128]{2,1,0:T(8,128)} %get-tuple-element.5) | copy-start | bytes 196612

commit v7 on v4

--- a/solution.py
+++ b/solution.py
@@ -152,7 +152,7 @@
     ]
     around_m = [(q, piece_copy(q, m, H, m, t, u_send, m_recv)) for q in pieces]
     down = [(q, piece_copy(q, c, 0, m, t - 1, m_send, m_recv)) for q in pieces]
-    chunks = 4
+    chunks = 2
     half = bx // chunks
     mains = [
         pltpu.make_async_remote_copy(

time: 36.4 us -> 36.9 us (1.014)
  Pallas kernels: 32.9 us -> 33.4 us
    pallas_call x1, Pallas kernels: 32.9 us -> 33.4 us  [shards(): pl.pallas_call(functools.partial(kernel, nt, ns), out_shape=(jax.ShapeDty...]
where the time goes in v7:
time: 36.9 us; the launch traced here: 36.3 us
  Pallas kernels  33.4 us (91%)
  local copies, waits for them, and re-layouts  2.23 us (6%)
  between operations  0.65 us (2%)
    pallas_call x1, Pallas kernels, shards(): pl.pallas_call(functools.partial(kernel, nt, ns), out_shape=(jax.ShapeDty...  33.4 us
    unnamed x4, local copies, waits for them, and re-layouts  2.23 us

profile of v7, /device:TPU:0, one launch (start us, length us, event | category | flops | bytes accessed | tf_op | source)
XLA Modules:
  0.0 36.3 jit_solution(3043538759324783335)
XLA Ops:
  0.6 33.4 %shard_map.77 = (f32[2,8,16,128]{3,2,1,0:T(8,128)}, f32[8,16,128]{2,1,0:T(8,128)}) custom-call(f32[2,8,16,128]{3,2,1,0:T(8,128)} %src_hbm.1, f32[2,8,16,128]{3,2,1,0:T(8,128)} %fs_hbm.1, f32[8,16,128]{2,1,0:T(8,128)} %term_hbm.1, f32[8,16,128]{2,1,0:T(8,128)} %damp_hbm.1, f32[8]{0:T(128)} %stiff_hbm.1, s32[2,1,2]{2,1,0:T(1,128)} %reg_hbm.1), custom_call_target="tpu_custom_call" | custom-call | tf_op jit(solution)/shard_map/pallas_call | solution.py:361
  34.0 0.0 copy-start
  34.0 1.6 %copy.10 = f32[2,8,16,128]{3,2,1,0:T(8,128)} copy(f32[2,8,16,128]{3,2,1,0:T(8,128)} %get-tuple-element.4) | data formatting | bytes 262144
  35.6 0.0 copy-done
  35.6 0.6 %copy.11 = f32[8,16,128]{2,1,0:T(8,128)} copy(f32[8,16,128]{2,1,0:T(8,128)S(1)} %copy-done) | data formatting | bytes 131072
Async XLA Ops:
  34.0 1.6 %copy-start = (f32[8,16,128]{2,1,0:T(8,128)S(1)}, f32[8,16,128]{2,1,0:T(8,128)}, u32[]{:S(2)}) copy-start(f32[8,16,128]{2,1,0:T(8,128)} %get-tuple-element.5) | copy-start | bytes 196612

commit v8 on v7

--- a/solution.py
+++ b/solution.py
@@ -152,7 +152,7 @@
     ]
     around_m = [(q, piece_copy(q, m, H, m, t, u_send, m_recv)) for q in pieces]
     down = [(q, piece_copy(q, c, 0, m, t - 1, m_send, m_recv)) for q in pieces]
-    chunks = 2
+    chunks = 8
     half = bx // chunks
     mains = [
         pltpu.make_async_remote_copy(
@@ -384,7 +384,7 @@
             pltpu.VMEM(block, f32),
             pltpu.VMEM((2,) + block, f32),
             dma((6,)), dma((3,)), dma((5,)), dma((5,)), dma((5,)), dma((5,)), dma((5,)),
-            dma((9,)), dma((9,)), dma((1,)), dma((1,)), dma((nt,)), dma((2,)),
+            dma((13,)), dma((13,)), dma((1,)), dma((1,)), dma((nt,)), dma((2,)),
         ],
         compiler_params=pltpu.CompilerParams(
             collective_id=0, has_side_effects=True, vmem_limit_bytes=64 * 1024 * 1024

time: 36.9 us -> 36.1 us (0.978)
  Pallas kernels: 33.4 us -> 32.8 us
    pallas_call x1, Pallas kernels: 33.4 us -> 32.8 us  [shards(): pl.pallas_call(functools.partial(kernel, nt, ns), out_shape=(jax.ShapeDty...]
where the time goes in v8:
time: 36.1 us; the launch traced here: 35.6 us
  Pallas kernels  32.8 us (91%)
  local copies, waits for them, and re-layouts  2.23 us (6%)
  between operations  0.65 us (2%)
    pallas_call x1, Pallas kernels, shards(): pl.pallas_call(functools.partial(kernel, nt, ns), out_shape=(jax.ShapeDty...  32.8 us
    unnamed x4, local copies, waits for them, and re-layouts  2.23 us

profile of v8, /device:TPU:0, one launch (start us, length us, event | category | flops | bytes accessed | tf_op | source)
XLA Modules:
  0.0 35.6 jit_solution(3186437366719315415)
XLA Ops:
  0.6 32.8 %shard_map.77 = (f32[2,8,16,128]{3,2,1,0:T(8,128)}, f32[8,16,128]{2,1,0:T(8,128)}) custom-call(f32[2,8,16,128]{3,2,1,0:T(8,128)} %src_hbm.1, f32[2,8,16,128]{3,2,1,0:T(8,128)} %fs_hbm.1, f32[8,16,128]{2,1,0:T(8,128)} %term_hbm.1, f32[8,16,128]{2,1,0:T(8,128)} %damp_hbm.1, f32[8]{0:T(128)} %stiff_hbm.1, s32[2,1,2]{2,1,0:T(1,128)} %reg_hbm.1), custom_call_target="tpu_custom_call" | custom-call | tf_op jit(solution)/shard_map/pallas_call | solution.py:361
  33.4 0.0 copy-start
  33.4 1.6 %copy.10 = f32[2,8,16,128]{3,2,1,0:T(8,128)} copy(f32[2,8,16,128]{3,2,1,0:T(8,128)} %get-tuple-element.4) | data formatting | bytes 262144
  35.0 0.0 copy-done
  35.0 0.6 %copy.11 = f32[8,16,128]{2,1,0:T(8,128)} copy(f32[8,16,128]{2,1,0:T(8,128)S(1)} %copy-done) | data formatting | bytes 131072
Async XLA Ops:
  33.4 1.6 %copy-start = (f32[8,16,128]{2,1,0:T(8,128)S(1)}, f32[8,16,128]{2,1,0:T(8,128)}, u32[]{:S(2)}) copy-start(f32[8,16,128]{2,1,0:T(8,128)} %get-tuple-element.5) | copy-start | bytes 196612
